TPU v7x, 128 devices: a whole 4x4x4 slice. The times are simulated.
128 devices in a mesh: row: 16 (over z, y), col: 8 (over x, core).
Axes of the slice: x: 4, y: 4, z: 4, core: 2. Of those that a mesh axis runs over, the one named last changes fastest.
Arguments:
- front: bfloat16 [32768, 32768], P('row', 'col'), may hold values from -0.0625 to 0.0625
- tile_mask: int32 [128, 128], P('row', 'col'), may hold values 0 or 1
- probes: bfloat16 [32768, 256], P(('col', 'row')), may hold values from -6 to 6
- coupling: float32 [32768, 256], P(('row', 'col')), may hold values from -0.375 to 0.375
Outputs:
- leaf_basis: float32 [32768, 256], P(('row', 'col'))
- upper_transfer: float32 [6, 32768, 256], P(None, ('row', 'col'))
Inputs may be any that keep to these rules, and one draw needn't show every extreme that they name: `tile_mask`: 1 where a tile of the front is present, 0 where it is absent.
All inputs are finite; a program needn't handle non-finite values. No bound on the sum of `tile_mask` on one device may be relied on, other than what follows from the above.
Results may differ from a plain program's by a relative error of at most 0.0003.
Values may be sent and summed in bfloat16 or wider, within the bound.
A program may use at most 128 MiB of HBM per device.

v0:
```python
import jax
import jax.numpy as jnp
from jax import lax
from jax.sharding import PartitionSpec as P


def from_root(x, axis, root):
    mine = lax.axis_index(axis) == root
    return lax.psum(jnp.where(mine, x, jnp.zeros_like(x)), axis)


def from_partner(value, axis, distance):
    mask = 2**distance
    pairs = [(source, source ^ mask) for source in range(lax.axis_size(axis))]
    return lax.ppermute(value, axis, pairs)


def matmul_high(left, right):
    return jnp.matmul(left, right, precision=lax.Precision.HIGHEST)


def transpose_last(array):
    return jnp.swapaxes(array, -1, -2)


def merge_pair(top_node, bottom_node, level_index):
    top_s, top_w, top_p = top_node
    bottom_s, bottom_w, bottom_p = bottom_node
    if level_index > 1:
        factor = 2.0 ** (-(level_index - 1) / 2.0)
        top_s = top_s - factor * matmul_high(top_p, bottom_w)
        bottom_s = bottom_s - factor * matmul_high(bottom_p, top_w)
    stacked = jnp.concatenate([top_s, bottom_s], axis=-2)
    gram_matrix = matmul_high(transpose_last(stacked), stacked)
    probe_count = gram_matrix.shape[-1]
    shift_value = 0.001 * (jnp.trace(gram_matrix, axis1=-2, axis2=-1) / probe_count + 1e-06)
    gram_matrix = gram_matrix + shift_value[..., None, None] * jnp.eye(
        probe_count, dtype=jnp.float32
    )
    lower_factor = jnp.linalg.cholesky(gram_matrix)
    basis_rows = jax.scipy.linalg.solve_triangular(
        lower_factor, transpose_last(stacked), lower=True
    )
    new_w = matmul_high(basis_rows, jnp.concatenate([top_w, bottom_w], axis=-2))
    row_total = top_s.shape[-2]
    top_half = transpose_last(basis_rows[..., :row_total])
    bottom_half = transpose_last(basis_rows[..., row_total:])
    return ((transpose_last(lower_factor), new_w, top_p + bottom_p), top_half, bottom_half)


def pair_step(node_state, partner, side_bit, level_index):
    is_top = side_bit == 0
    top_node = tuple((jnp.where(is_top, mine, other) for mine, other in zip(node_state, partner)))
    bottom_node = tuple(
        (jnp.where(is_top, other, mine) for mine, other in zip(node_state, partner))
    )
    parent, top_half, bottom_half = merge_pair(top_node, bottom_node, level_index)
    return (parent, jnp.where(is_top, top_half, bottom_half))


def pack_state(node_state):
    return jnp.concatenate(node_state, axis=0)


def unpack_state(packed, sample_rows, probe_rows):
    return (
        packed[:sample_rows],
        packed[sample_rows : sample_rows + probe_rows],
        packed[sample_rows + probe_rows :],
    )


def shards(front, tile_mask, probes, coupling):
    col_count = lax.axis_size("col")
    row_count = lax.axis_size("row")
    row_index = lax.axis_index("row")
    col_index = lax.axis_index("col")
    leaf_rows = front.shape[0] // col_count
    probe_count = probes.shape[1]
    col_levels = col_count.bit_length() - 1
    row_levels = row_count.bit_length() - 1
    probe_block = lax.all_gather(probes, "row", axis=0, tiled=True)
    tile_above = row_index * col_count + jnp.arange(col_count, dtype=jnp.int32)
    tile_across = col_index * row_count + jnp.arange(row_count, dtype=jnp.int32)
    keep_tiles = tile_mask * (tile_above[:, None] // 2 != tile_across[None, :] // 2).astype(
        jnp.int32
    )
    masked = (
        front.reshape(col_count, leaf_rows, row_count, leaf_rows)
        * keep_tiles.astype(jnp.bfloat16)[:, None, :, None]
    )
    partial_value = jnp.dot(
        masked.reshape(front.shape), probe_block, preferred_element_type=jnp.float32
    )
    sample = lax.psum_scatter(partial_value, "col", scatter_dimension=0, tiled=True)
    offset = row_index * col_count % row_count * leaf_rows
    root_col = row_index * col_count // row_count
    offered = lax.dynamic_slice_in_dim(probe_block, offset, col_count * leaf_rows, 0)
    group_probes = from_root(offered, "col", root_col)
    own_probe = lax.dynamic_slice_in_dim(group_probes, col_index * leaf_rows, leaf_rows, 0).astype(
        jnp.float32
    )
    halves = []
    node_state = (sample, own_probe, coupling)
    for bit_index in range(col_levels):
        sample_rows = node_state[0].shape[0]
        probe_rows = node_state[1].shape[0]
        packed = from_partner(pack_state(node_state), "col", bit_index)
        partner = unpack_state(packed, sample_rows, probe_rows)
        node_state, own_half = pair_step(
            node_state, partner, col_index >> bit_index & 1, bit_index + 1
        )
        halves.append(own_half)
    for bit_index in range(row_levels):
        packed = from_partner(pack_state(node_state), "row", bit_index)
        partner = unpack_state(packed, probe_count, probe_count)
        node_state, own_half = pair_step(
            node_state, partner, row_index >> bit_index & 1, col_levels + bit_index + 1
        )
        halves.append(own_half)
    return (halves[0], jnp.stack(halves[1:], axis=0))


def solution(mesh):
    in_specs = (P("row", "col"), P("row", "col"), P(("col", "row"), None), P(("row", "col"), None))
    out_specs = (P(("row", "col"), None), P(None, ("row", "col"), None))
    return jax.shard_map(shards, mesh=mesh, in_specs=in_specs, out_specs=out_specs, check_vma=False)
```

profile of v0, /device:TPU:2, one launch (start us, length us, event | category | flops | bytes accessed | tf_op | source)
XLA Modules:
  0.0 792.1 jit_solution(5654352829318826100)
XLA Ops:
  22.2 38.7 %all-gather.2.cloned.1.call-done = bf16[4096,256]{0,1:T(8,128)(2,1)} async-done(((bf16[256,256]{0,1:T(8,128)(2,1)}), bf16[4096,256]{0,1:T(8,128)(2,1)}) %all-gather.2.cloned.1.call-update) | async-done | bytes 2097168 | tf_op jit(solution)/shard_map/all_gather | solution.py:82
  63.5 16.6 %fusion = f32[2048,256]{0,1:T(8,128)} fusion(bf16[4096,256]{0,1:T(8,128)(2,1)S(1)} %copy-done.21, bf16[2048,4096]{1,0:T(8,128)(2,1)} %param.7, bf16[2048,4096]{1,0:T(8,128)(2,1)} %bitcast.284), kind=kOutput, calls=%fused_computation.14 | convolution fusion | flops 4303355904 | bytes 37748736 | tf_op jit(solution)/shard_map/dot_general | solution.py:92
  81.2 41.9 %all-reduce.3.cloned.1.call-done = bf16[2048,256]{0,1:T(8,128)(2,1)} async-done(((bf16[2048,256]{0,1:T(8,128)(2,1)}), bf16[2048,256]{0,1:T(8,128)(2,1)}) %all-reduce.3.cloned.1.call-update) | async-done | bytes 1048592 | tf_op jit(solution)/shard_map/psum | solution.py:9
  124.1 33.5 %reduce-scatter.2.cloned.1.call-done = f32[256,256]{0,1:T(8,128)} async-done(((f32[2048,256]{0,1:T(8,128)}), f32[256,256]{0,1:T(8,128)}) %reduce-scatter.2.cloned.1.call-update) | async-done | bytes 262160 | tf_op jit(solution)/shard_map/reduce_scatter | solution.py:95
  164.4 11.7 %cholesky.340 = f32[128,128]{1,0:T(8,128)S(1)} custom-call(f32[128,128]{1,0:T(8,128)S(1)} %cholesky.574), custom_call_target="Cholesky" | custom-call | tf_op jit(solution)/shard_map/jit(cholesky)/cholesky | solution.py:40
  186.7 11.7 %cholesky.357 = f32[128,128]{1,0:T(8,128)S(1)} custom-call(f32[128,128]{1,0:T(8,128)S(1)} %convolution_subtract_fusion.13), custom_call_target="Cholesky" | custom-call | tf_op jit(solution)/shard_map/jit(cholesky)/cholesky | solution.py:40
  204.8 19.7 %custom-call.24 = f32[2,128,128]{1,2,0:T(8,128)S(1)} custom-call(f32[2,128,128]{2,1,0:T(8,128)S(1)} %get-tuple-element.48), custom_call_target="InvertDiagBlocksLowerTriangular" | custom-call | tf_op jit(solution)/shard_map/jit(_solve_triangular)/triangular_solve | solution.py:41
  231.0 17.8 %collective-permute-done.1 = f32[768,256]{0,1:T(8,128)S(1)} collective-permute-done((f32[768,256]{0,1:T(8,128)S(1)}, f32[768,256]{0,1:T(8,128)S(1)}, u32[]{:S(2)}, u32[]{:S(2)}) %collective-permute-start.1) | collective-permute-done | bytes 786464 | tf_op jit(solution)/shard_map/ppermute | solution.py:15
  252.0 11.7 %cholesky.374 = f32[128,128]{1,0:T(8,128)S(1)} custom-call(f32[128,128]{1,0:T(8,128)S(1)} %cholesky.577), custom_call_target="Cholesky" | custom-call | tf_op jit(solution)/shard_map/jit(cholesky)/cholesky | solution.py:40
  274.4 11.7 %cholesky.391 = f32[128,128]{1,0:T(8,128)S(1)} custom-call(f32[128,128]{1,0:T(8,128)S(1)} %convolution_subtract_fusion.12), custom_call_target="Cholesky" | custom-call | tf_op jit(solution)/shard_map/jit(cholesky)/cholesky | solution.py:40
  293.2 19.7 %custom-call.26 = f32[2,128,128]{1,2,0:T(8,128)S(1)} custom-call(f32[2,128,128]{2,1,0:T(8,128)S(1)} %get-tuple-element.49), custom_call_target="InvertDiagBlocksLowerTriangular" | custom-call | tf_op jit(solution)/shard_map/jit(_solve_triangular)/triangular_solve | solution.py:41
  316.3 19.6 %collective-permute-done.2 = f32[768,256]{0,1:T(8,128)} collective-permute-done((f32[768,256]{0,1:T(8,128)S(1)}, f32[768,256]{0,1:T(8,128)}, u32[]{:S(2)}, u32[]{:S(2)}) %collective-permute-start.2) | collective-permute-done | bytes 786464 | tf_op jit(solution)/shard_map/ppermute | solution.py:15
  342.0 11.7 %cholesky.408 = f32[128,128]{1,0:T(8,128)S(1)} custom-call(f32[128,128]{1,0:T(8,128)S(1)} %cholesky.580), custom_call_target="Cholesky" | custom-call | tf_op jit(solution)/shard_map/jit(cholesky)/cholesky | solution.py:40
  364.3 11.7 %cholesky.425 = f32[128,128]{1,0:T(8,128)S(1)} custom-call(f32[128,128]{1,0:T(8,128)S(1)} %convolution_subtract_fusion.11), custom_call_target="Cholesky" | custom-call | tf_op jit(solution)/shard_map/jit(cholesky)/cholesky | solution.py:40
  383.4 19.7 %custom-call.28 = f32[2,128,128]{1,2,0:T(8,128)S(1)} custom-call(f32[2,128,128]{2,1,0:T(8,128)S(1)} %get-tuple-element.50), custom_call_target="InvertDiagBlocksLowerTriangular" | custom-call | tf_op jit(solution)/shard_map/jit(_solve_triangular)/triangular_solve | solution.py:41
  406.8 16.9 %collective-permute-done.3 = f32[768,256]{0,1:T(8,128)} collective-permute-done((f32[768,256]{0,1:T(8,128)S(1)}, f32[768,256]{0,1:T(8,128)}, u32[]{:S(2)}, u32[]{:S(2)}) %collective-permute-start.3) | collective-permute-done | bytes 786464 | tf_op jit(solution)/shard_map/ppermute | solution.py:15
  430.5 11.7 %cholesky.442 = f32[128,128]{1,0:T(8,128)S(1)} custom-call(f32[128,128]{1,0:T(8,128)S(1)} %cholesky.583), custom_call_target="Cholesky" | custom-call | tf_op jit(solution)/shard_map/jit(cholesky)/cholesky | solution.py:40
  475.0 19.7 %custom-call.30 = f32[2,128,128]{1,2,0:T(8,128)S(1)} custom-call(f32[2,128,128]{2,1,0:T(8,128)S(1)} %get-tuple-element.51), custom_call_target="InvertDiagBlocksLowerTriangular" | custom-call | tf_op jit(solution)/shard_map/jit(_solve_triangular)/triangular_solve | solution.py:41
  502.7 16.1 %collective-permute-done.4 = f32[768,256]{0,1:T(8,128)} collective-permute-done((f32[768,256]{0,1:T(8,128)}, f32[768,256]{0,1:T(8,128)}, u32[]{:S(2)}, u32[]{:S(2)}) %collective-permute-start.4) | collective-permute-done | bytes 786464 | tf_op jit(solution)/shard_map/ppermute | solution.py:15
  570.8 19.7 %custom-call.32 = f32[2,128,128]{1,2,0:T(8,128)S(1)} custom-call(f32[2,128,128]{2,1,0:T(8,128)S(1)} %get-tuple-element.52), custom_call_target="InvertDiagBlocksLowerTriangular" | custom-call | tf_op jit(solution)/shard_map/jit(_solve_triangular)/triangular_solve | solution.py:41
  600.3 15.2 %collective-permute-done.5 = f32[768,256]{0,1:T(8,128)} collective-permute-done((f32[768,256]{0,1:T(8,128)}, f32[768,256]{0,1:T(8,128)}, u32[]{:S(2)}, u32[]{:S(2)}) %collective-permute-start.5) | collective-permute-done | bytes 786464 | tf_op jit(solution)/shard_map/ppermute | solution.py:15
  670.3 20.5 %custom-call.34 = f32[2,128,128]{1,2,0:T(8,128)S(1)} custom-call(f32[2,128,128]{2,1,0:T(8,128)} %copy-done.23), custom_call_target="InvertDiagBlocksLowerTriangular" | custom-call | tf_op jit(solution)/shard_map/jit(_solve_triangular)/triangular_solve | solution.py:41
  744.7 11.7 %cholesky.561 = f32[128,128]{1,0:T(8,128)S(1)} custom-call(f32[128,128]{1,0:T(8,128)S(1)} %convolution_subtract_fusion.7), custom_call_target="Cholesky" | custom-call | tf_op jit(solution)/shard_map/jit(cholesky)/cholesky | solution.py:40
  763.4 19.7 %custom-call.36 = f32[2,128,128]{1,2,0:T(8,128)S(1)} custom-call(f32[2,128,128]{2,1,0:T(8,128)S(1)} %get-tuple-element.54), custom_call_target="InvertDiagBlocksLowerTriangular" | custom-call | tf_op jit(solution)/shard_map/jit(_solve_triangular)/triangular_solve | solution.py:41
  (320 shorter events, 341.8 us)
Async XLA Ops:
  7.2 53.7 %all-gather.2.cloned.1.call-start = ((), (), s32[]{:S(2)}) async-start(), calls=%async_computation.1 | async-start | bytes 2228224 | tf_op jit(solution)/shard_map/all_gather | solution.py:82
  8.9 114.3 %all-reduce.3.cloned.1.call-start = ((), (), s32[]{:S(2)}) async-start(), calls=%async_computation.3 | async-start | bytes 2097152 | tf_op jit(solution)/shard_map/psum | solution.py:9
  60.9 2.6 copy-start.21
  63.5 94.1 %reduce-scatter.2.cloned.1.call-start = ((), (), s32[]{:S(2)}) async-start(), calls=%async_computation.2 | async-start | bytes 2359296 | tf_op jit(solution)/shard_map/reduce_scatter | solution.py:95
  157.6 3.6 copy-start.9
  158.7 2.5 collective-permute-start
  226.7 22.1 %collective-permute-start.1 = (f32[768,256]{0,1:T(8,128)S(1)}, f32[768,256]{0,1:T(8,128)S(1)}, u32[]{:S(2)}, u32[]{:S(2)}) collective-permute-start(f32[768,256]{0,1:T(8,128)S(1)} %pad_maximum_fusion.1), channel_id=1, source_target_pairs={{0,2},{1,3},{2,0},{3,1},{4,6},{5,7},{6,4},{7,5},{8,10},{9,11},{10,... | collective-permute-start | bytes 2359304 | tf_op jit(solution)/shard_map/ppermute | solution.py:15
  249.8 2.0 copy-start.11
  251.8 22.5 %copy-start.12 = (f32[256,256]{0,1:T(8,128)S(1)}, f32[256,256]{0,1:T(8,128)}, u32[]{:S(2)}) copy-start(f32[256,256]{0,1:T(8,128)} %copy-done.11) | copy-start | bytes 786436
  315.1 20.8 %collective-permute-start.2 = (f32[768,256]{0,1:T(8,128)S(1)}, f32[768,256]{0,1:T(8,128)}, u32[]{:S(2)}, u32[]{:S(2)}) collective-permute-start(f32[768,256]{0,1:T(8,128)S(1)} %pad_maximum_fusion.2), channel_id=1, source_target_pairs={{0,4},{1,5},{2,6},{3,7},{4,0},{5,1},{6,2},{7,3},{8,12},{9,13},{10,... | collective-permute-start | bytes 2359304 | tf_op jit(solution)/shard_map/ppermute | solution.py:15
  405.3 18.4 %collective-permute-start.3 = (f32[768,256]{0,1:T(8,128)S(1)}, f32[768,256]{0,1:T(8,128)}, u32[]{:S(2)}, u32[]{:S(2)}) collective-permute-start(f32[768,256]{0,1:T(8,128)S(1)} %pad_maximum_fusion.3), channel_id=1, source_target_pairs={{0,8},{8,0},{16,24},{24,16},{32,40},{40,32},{48,56},{56,48},{64,72... | collective-permute-start | bytes 2359304 | tf_op jit(solution)/shard_map/ppermute | solution.py:15
  430.5 11.8 %copy-start.18 = (f32[256,256]{1,0:T(8,128)}, f32[256,256]{1,0:T(8,128)S(1)}, u32[]{:S(2)}) copy-start(f32[256,256]{1,0:T(8,128)S(1)} %fusion.90) | copy-start | bytes 786436
  498.8 3.9 copy-start.7
  499.8 19.1 %collective-permute-start.4 = (f32[768,256]{0,1:T(8,128)}, f32[768,256]{0,1:T(8,128)}, u32[]{:S(2)}, u32[]{:S(2)}) collective-permute-start(f32[768,256]{0,1:T(8,128)} %pad_maximum_fusion.4), channel_id=1, source_target_pairs={{0,16},{8,24},{16,0},{24,8},{32,48},{40,56},{48,32},{56,40},{64,80... | collective-permute-start | bytes 2359304 | tf_op jit(solution)/shard_map/ppermute | solution.py:15
  520.0 4.3 copy-start.3
  521.6 1.6 copy-start.14
  598.8 16.6 %collective-permute-start.5 = (f32[768,256]{0,1:T(8,128)}, f32[768,256]{0,1:T(8,128)}, u32[]{:S(2)}, u32[]{:S(2)}) collective-permute-start(f32[768,256]{0,1:T(8,128)} %pad_maximum_fusion.5), channel_id=1, source_target_pairs={{0,32},{8,40},{16,48},{24,56},{32,0},{40,8},{48,16},{56,24},{64,96... | collective-permute-start | bytes 2359304 | tf_op jit(solution)/shard_map/ppermute | solution.py:15
  616.7 4.5 copy-start.4
  616.7 4.4 copy-start.5
  618.3 1.6 copy-start.16
  619.9 1.2 copy-start.17
  623.6 11.8 %copy-start.20 = (f32[256,256]{1,0:T(8,128)}, f32[256,256]{1,0:T(8,128)S(1)}, u32[]{:S(2)}) copy-start(f32[256,256]{1,0:T(8,128)S(1)} %fusion.88) | copy-start | bytes 786436
  661.3 2.7 copy-start.10
  700.0 17.2 %collective-permute-start.6 = (f32[768,256]{0,1:T(8,128)}, f32[768,256]{0,1:T(8,128)}, u32[]{:S(2)}, u32[]{:S(2)}) collective-permute-start(f32[768,256]{0,1:T(8,128)} %pad_maximum_fusion.6), channel_id=1, source_target_pairs={{0,64},{8,72},{16,80},{24,88},{32,96},{40,104},{48,112},{56,120},{... | collective-permute-start | bytes 2359304 | tf_op jit(solution)/shard_map/ppermute | solution.py:15
  (11 other events, 9.5 us)
Sparse Core Ops, SparseCore 0:
  10.7 50.1 all-gather.1
  63.8 59.3 all-reduce.2
  125.6 31.9 reduce-scatter.1
where the time goes:
time: 799 us; the launch traced here: 792 us
  other arithmetic  405 us (51%)
  waiting for transfers between devices  213 us (27%)
  matrix products  74.6 us (9%)
  local copies, waits for them, and re-layouts  53.6 us (7%)
  between operations  30 us (4%)
  starting transfers between devices  14.9 us (2%)
    another operation x48, other arithmetic, merge_pair(): lower_factor = jnp.linalg.cholesky(gram_matrix)  242 us
    another operation x9, other arithmetic, merge_pair(): jax.scipy.linalg.solve_triangular(lower_factor, transpose_last(stacked),...  139 us
    ppermute x7, waiting for transfers between devices, from_partner(): return lax.ppermute(value, axis, pairs)  99 us
    psum x1, waiting for transfers between devices, from_root(): return lax.psum(jnp.where(mine, x, jnp.zeros_like(x)), axis)  41.9 us
    all_gather x1, waiting for transfers between devices, shards(): probe_block = lax.all_gather(probes, 'row', axis=0, tiled=True)  38.7 us
    reduce_scatter x1, waiting for transfers between devices, shards(): lax.psum_scatter(partial_value, 'col', scatter_dimension=0, tiled=True)  33.5 us
    dot_general x25, matrix products, matmul_high(): return jnp.matmul(left, right, precision=lax.Precision.HIGHEST)  30.3 us
    another operation x57, local copies, waits for them, and re-layouts, merge_pair(): jax.scipy.linalg.solve_triangular(lower_factor, transpose_last(stacked),...  29.9 us
  transfers between devices with their start and end apart: 10, of which 10 were waited for; matrix products, arithmetic and copies ran while one was open for 4% of the time, Pallas kernels for 0%

commit v1 on v0

v1 whole, which is shorter than its diff:
```python
import jax
import jax.numpy as jnp
from jax import lax
from jax.experimental import pallas as pl
from jax.experimental.pallas import tpu as pltpu
from jax.sharding import PartitionSpec as P

F32=jnp.float32; BF=jnp.bfloat16

def split(x):
    h=x.astype(BF); l=(x-h.astype(F32)).astype(BF); return h,l
def dg(a,b,dims):
    return lax.dot_general(a,b,(dims,((),())),preferred_element_type=F32)
NN=((1,),(0,)); NT=((1,),(1,)); TN=((0,),(0,))
def dot3(a,b,dims=NN):
    ah,al=a if isinstance(a,tuple) else split(a)
    bh,bl=b if isinstance(b,tuple) else split(b)
    return dg(ah,bh,dims)+(dg(ah,bl,dims)+dg(al,bh,dims))

def lanes(v,c): return jnp.broadcast_to(v[:,c:c+1],(8,128))
def subs(v,i): return jnp.broadcast_to(v[i:i+1,:],(8,128))

def factor64(E,off):
    sub=lax.broadcasted_iota(jnp.int32,(8,128),0)
    E=list(E); X=[]
    for p in range(8):
        row=[subs(E[p],i) for i in range(8)]
        a={}
        for i in range(8):
            for j in range(i,8):
                a[i,j]=lanes(row[i],off+8*p+j)
        V={}
        for n in range(p+1,8):
            V[n]=[lanes(E[n],off+8*p+k) for k in range(8)]
        out=[None]*8
        for m in range(4):
            P,Q=2*m,2*m+1
            aa,bb,cc=a[P,P],a[P,Q],a[Q,Q]
            det=aa*cc-bb*bb
            r=1.0/det
            ra=cc*r; rb=bb*r; rc=aa*r
            yp=ra*row[P]-rb*row[Q]
            yq=rc*row[Q]-rb*row[P]
            t={}
            for i in range(Q+1,8):
                u,v=a[P,i],a[Q,i]
                tp=(cc*u-bb*v)*r
                tq=(aa*v-bb*u)*r
                t[i]=(tp,tq)
                for j in range(i,8):
                    a[i,j]=a[i,j]-(tp*a[P,j]+tq*a[Q,j])
                row[i]=row[i]-(tp*row[P]+tq*row[Q])
            for n in range(p+1,8):
                vp,vq=V[n][P],V[n][Q]
                for i in range(Q+1,8):
                    tp,tq=t[i]
                    V[n][i]=V[n][i]-(tp*vp+tq*vq)
                E[n]=E[n]-(vp*yp+vq*yq)
            sp=lax.rsqrt(aa)
            ba=bb/aa
            sq=lax.rsqrt(cc-bb*ba)
            out[P]=sp*row[P]
            out[Q]=sq*(row[Q]-ba*row[P])
        x=out[0]
        for i in range(1,8): x=jnp.where(sub==i,out[i],x)
        X.append(x)
    return X

def eliminate(T):
    lane=lax.broadcasted_iota(jnp.int32,(8,128),1)
    sub=lax.broadcasted_iota(jnp.int32,(8,128),0)
    for k in range(4):
        r0=64*k; off=r0%128; g0=r0-off
        E=[]
        for p in range(8):
            v=T[r0+8*p:r0+8*p+8,g0:g0+128]
            inb=(lane>=off)&(lane<off+64)
            eye=(lane==(64-off)+8*p+sub).astype(F32)
            E.append(jnp.where(inb,v,eye))
        X=factor64(E,off)
        Xm=jnp.concatenate(X,0)
        Li=Xm[:,64-off:128-off]
        Lh,Ll=split(Li)
        Tr=T[r0:r0+64,:]
        if k<3:
            Z=dot3(T[r0+64:256,r0:r0+64],(Lh,Ll),NT)
        Xk=dot3((Lh,Ll),Tr)
        if k<3:
            T[r0+64:256,:]=T[r0+64:256,:]-dot3(Z,Xk)
        T[r0:r0+64,:]=Xk
        for p in range(8):
            rr=r0+8*p
            c=lax.broadcasted_iota(jnp.int32,(8,256),1); rw=lax.broadcasted_iota(jnp.int32,(8,256),0)+rr
            T[rr:rr+8,0:256]=jnp.where(c>=rw,T[rr:rr+8,0:256],0.0)
            T[rr:rr+8,512:768]=jnp.where(c<=rw,T[rr:rr+8,512:768],0.0)


def level_kernel(factor, s_ref, w_ref, p_ref, other_ref, otherp_ref, snew_ref, wnew_ref, q_ref, T):
    s, w = s_ref[...], w_ref[...]
    so, wo = other_ref[0:256, :], other_ref[256:512, :]
    if factor is not None:
        s = s - factor * dot3(p_ref[...], wo)
        so = so - factor * dot3(otherp_ref[...], w)
    mt = split(jnp.concatenate([s, so], axis=0).T)
    gram = dot3(mt, jnp.concatenate([s, so], axis=0))
    cross = dot3(mt, jnp.concatenate([w, wo], axis=0))
    rows = lax.broadcasted_iota(jnp.int32, (256, 256), 0)
    columns = lax.broadcasted_iota(jnp.int32, (256, 256), 1)
    eye = rows == columns
    trace = jnp.sum(jnp.where(eye, gram, 0.0))
    shift = 0.001 * (trace / 256.0 + 1e-6)
    T[:, 0:256] = gram + jnp.where(eye, shift, 0.0)
    T[:, 256:512] = cross
    T[:, 512:768] = jnp.where(eye, 1.0, 0.0)
    eliminate(T)
    snew_ref[...] = T[:, 0:256]
    wnew_ref[...] = T[:, 256:512]
    q_ref[...] = dot3(s, T[:, 512:768], NT)


def level_step(factor, s, w, p, other, other_p):
    square = jax.ShapeDtypeStruct((256, 256), F32)
    vmem = pl.BlockSpec(memory_space=pltpu.VMEM)
    return pl.pallas_call(
        lambda *refs: level_kernel(factor, *refs),
        out_shape=[square] * 3,
        in_specs=[vmem] * 5,
        out_specs=[vmem] * 3,
        scratch_shapes=[pltpu.VMEM((256, 768), F32)],
        compiler_params=pltpu.CompilerParams(vmem_limit_bytes=32 << 20),
        cost_estimate=pl.CostEstimate(flops=1 << 30, bytes_accessed=1 << 21, transcendentals=0),
    )(s, w, p, other, other_p)


def exchange(value, level):
    axis, bit, count = ("col", level, 8) if level < 3 else ("row", level - 3, 16)
    return lax.ppermute(value, axis, [(i, i ^ (1 << bit)) for i in range(count)])


def shards(front, tile_mask, probes, coupling):
    row_index = lax.axis_index("row")
    col_index = lax.axis_index("col")
    leaf_probe = lax.ppermute(
        probes, ("row", "col"), [((d % 16) * 8 + d // 16, d) for d in range(128)]
    )
    probe_block = lax.all_gather(probes, "row", axis=0, tiled=True)
    tile_above = row_index * 8 + jnp.arange(8, dtype=jnp.int32)
    tile_across = col_index * 16 + jnp.arange(16, dtype=jnp.int32)
    keep = tile_mask * (tile_above[:, None] // 2 != tile_across[None, :] // 2).astype(jnp.int32)
    masked = front.reshape(8, 256, 16, 256) * keep.astype(BF)[:, None, :, None]
    partial = jnp.dot(masked.reshape(front.shape), probe_block, preferred_element_type=F32)
    sample = lax.psum_scatter(partial, "col", scatter_dimension=0, tiled=True)
    others_p, p = [], coupling
    sums_p = [coupling]
    for level in range(7):
        others_p.append(exchange(sums_p[-1], level))
        sums_p.append(sums_p[-1] + others_p[-1])
    s, w = sample, leaf_probe.astype(F32)
    halves = []
    for level in range(7):
        other = exchange(jnp.concatenate([s, w], axis=0), level)
        factor = None if level == 0 else 2.0 ** (-level / 2.0)
        s, w, q = level_step(factor, s, w, sums_p[level], other, others_p[level])
        halves.append(q)
    return halves[0], jnp.stack(halves[1:], axis=0)


def solution(mesh):
    in_specs = (P("row", "col"), P("row", "col"), P(("col", "row"), None), P(("row", "col"), None))
    out_specs = (P(("row", "col"), None), P(None, ("row", "col"), None))
    return jax.shard_map(shards, mesh=mesh, in_specs=in_specs, out_specs=out_specs, check_vma=False)
```

time: 799 us -> 307 us (0.38)
  other arithmetic: 405 us -> 13.2 us
  Pallas kernels: 0 us -> 63.8 us
  waiting for transfers between devices: 213 us -> 152 us
  matrix products: 74.6 us -> 17.8 us
  local copies, waits for them, and re-layouts: 53.6 us -> 15.5 us
  between operations: 30 us -> 14.8 us
  starting transfers between devices: 14.9 us -> 24.4 us
    another operation x58 -> x0, other arithmetic: 381 us -> none  [the longest x48 242 us: merge_pair(): lower_factor = jnp.linalg.cholesky(gram_matrix)]
    pallas_call x0 -> x6, Pallas kernels: none -> 63.8 us  [level_step(): pl.pallas_call(lambda *refs: level_kernel(factor, *refs), out_shape=[squa...]
    psum x1 -> x0, waiting for transfers between devices: 41.9 us -> none  [from_root(): return lax.psum(jnp.where(mine, x, jnp.zeros_like(x)), axis)]
    another operation x83 -> x0, local copies, waits for them, and re-layouts: 30.7 us -> none  [the longest x57 29.9 us: merge_pair(): jax.scipy.linalg.solve_triangular(lower_factor, transpose_last(stacked),...]
    dot_general x25 -> x0, matrix products: 30.3 us -> none  [matmul_high(): return jnp.matmul(left, right, precision=lax.Precision.HIGHEST)]
    another operation x35 -> x0, matrix products: 27.7 us -> none  [the longest x21 18.7 us: merge_pair(): jax.scipy.linalg.solve_triangular(lower_factor, transpose_last(stacked),...]
    reduce_scatter x1, waiting for transfers between devices: 33.5 us -> 22.4 us  [shards(): sample = lax.psum_scatter(partial, 'col', scatter_dimension=0, tiled=True)]
    pallas_call x0 -> x1, other arithmetic: none -> 11 us  [level_step(): pl.pallas_call(lambda *refs: level_kernel(factor, *refs), out_shape=[squa...]
  transfers between devices with their start and end apart: 10 -> 17, of which waited for: 10 -> 10; matrix products, arithmetic and copies ran while one was open for 4% -> 5% of each run, Pallas kernels for 0% -> 7%
where the time goes in v1:
time: 307 us; the launch traced here: 301 us
  waiting for transfers between devices  152 us (50%)
  Pallas kernels  63.8 us (21%)
  starting transfers between devices  24.4 us (8%)
  matrix products  17.8 us (6%)
  local copies, waits for them, and re-layouts  15.5 us (5%)
  between operations  14.8 us (5%)
  other arithmetic  13.2 us (4%)
    ppermute x14, waiting for transfers between devices, exchange(): return lax.ppermute(value, axis, [(i, i ^ 1 << bit) for i in range(count)])  85.2 us
    pallas_call x6, Pallas kernels, level_step(): pl.pallas_call(lambda *refs: level_kernel(factor, *refs), out_shape=[squa...  63.8 us
    all_gather x1, waiting for transfers between devices, shards(): probe_block = lax.all_gather(probes, 'row', axis=0, tiled=True)  36.7 us
    reduce_scatter x1, waiting for transfers between devices, shards(): sample = lax.psum_scatter(partial, 'col', scatter_dimension=0, tiled=True)  22.4 us
    ppermute x14, starting transfers between devices, exchange(): return lax.ppermute(value, axis, [(i, i ^ 1 << bit) for i in range(count)])  21.2 us
    dot_general x1, matrix products, shards(): jnp.dot(masked.reshape(front.shape), probe_block, preferred_element_type=...  17.8 us
    unnamed x14, local copies, waits for them, and re-layouts  13.8 us
    pallas_call x1, other arithmetic, level_step(): pl.pallas_call(lambda *refs: level_kernel(factor, *refs), out_shape=[squa...  11 us
  transfers between devices with their start and end apart: 17, of which 10 were waited for; matrix products, arithmetic and copies ran while one was open for 5% of the time, Pallas kernels for 7%

profile of v1, /device:TPU:2, one launch (start us, length us, event | category | flops | bytes accessed | tf_op | source)
XLA Modules:
  0.0 301.3 jit_solution(5672833630896533615)
XLA Ops:
  10.5 10.7 %copy.6 = bf16[256,8,16,256]{3,1,2,0:T(8,128)(2,1)} copy(bf16[256,8,16,256]{3,2,1,0:T(8,128)(2,1)S(1)} %bitcast.18) | data formatting | bytes 33554432
  21.2 36.7 %all-gather.2.cloned.1.call-done = bf16[4096,256]{1,0:T(8,128)(2,1)} async-done(((bf16[256,256]{1,0:T(8,128)(2,1)}), bf16[4096,256]{1,0:T(8,128)(2,1)}) %all-gather.2.cloned.1.call-update) | async-done | bytes 2097168 | tf_op jit(solution)/shard_map/all_gather | solution.py:146
  57.8 17.8 %fusion = f32[2048,256]{1,0:T(8,128)} fusion(bf16[4096,256]{1,0:T(8,128)(2,1)} %all-gather.2.cloned.1.call-done, bf16[2048,4096]{1,0:T(8,128)(2,1)} %param.4, bf16[2048,4096]{1,0:T(8,128)(2,1)} %bitcast.19), kind=kOutput, calls=%fused_computation | convolution fusion | flops 4303355904 | bytes 37748736 | tf_op jit(solution)/shard_map/dot_general | solution.py:151
  76.5 3.1 %collective-permute-start = (bf16[256,256]{1,0:T(8,128)(2,1)S(1)}, bf16[256,256]{1,0:T(8,128)(2,1)S(1)}, u32[]{:S(2)}, u32[]{:S(2)}) collective-permute-start(bf16[256,256]{1,0:T(8,128)(2,1)S(1)} %copy-done.2), channel_id=1, source_target_pairs={{0,0},{8,1},{16,2},{24,3},{32,4},{40,5},{48,6},{56,7},{64,8},{72,9... | collective-permute-start | bytes 393224 | tf_op jit(solution)/shard_map/ppermute | solution.py:143
  79.6 6.8 %collective-permute-done = bf16[256,256]{1,0:T(8,128)(2,1)S(1)} collective-permute-done((bf16[256,256]{1,0:T(8,128)(2,1)S(1)}, bf16[256,256]{1,0:T(8,128)(2,1)S(1)}, u32[]{:S(2)}, u32[]{:S(2)}) %collective-permute-start) | collective-permute-done | bytes 131104 | tf_op jit(solution)/shard_map/ppermute | solution.py:143
  86.5 22.4 %reduce-scatter.2.cloned.1.call-done.refs_0_ = f32[256,256]{1,0:T(8,128)} async-done(((f32[2048,256]{1,0:T(8,128)}), f32[256,256]{1,0:T(8,128)}) %reduce-scatter.2.cloned.1.call-update) | async-done | bytes 262160 | tf_op jit(solution)/shard_map/reduce_scatter | solution.py:152
  113.2 10.9 %shard_map.59 = (f32[256,256]{1,0:T(8,128)S(1)}, f32[256,256]{1,0:T(8,128)S(1)}, f32[256,256]{1,0:T(8,128)}) custom-call(f32[256,256]{1,0:T(8,128)S(1)} %copy-done.1, f32[256,256]{1,0:T(8,128)S(1)} %convert_element_type.8.refs_1_, f32[256,256]{1,0:T(8,128)S(1)} %copy-done, f32[512,256]{1,0:T(8,128)S(1)} %collective-permute-done.1.refs_3_, ...), custom_call_target="tpu_custom_call" | custom-call | flops 1073741824 | bytes 2097152 | tf_op jit(solution)/shard_map/pallas_call | solution.py:124
  124.2 3.9 %collective-permute-start.3 = (f32[512,256]{1,0:T(8,128)S(1)}, f32[512,256]{1,0:T(8,128)S(1)}, u32[]{:S(2)}, u32[]{:S(2)}) collective-permute-start(f32[512,256]{1,0:T(8,128)S(1)} %pad_maximum_fusion.1), channel_id=1, source_target_pairs={{0,2},{1,3},{2,0},{3,1},{4,6},{5,7},{6,4},{7,5},{8,10},{9,11},{10,... | collective-permute-start | bytes 1572872 | tf_op jit(solution)/shard_map/ppermute | solution.py:137
  128.4 17.4 %collective-permute-done.4.refs_4_ = f32[256,256]{1,0:T(8,128)S(1)} collective-permute-done((f32[256,256]{1,0:T(8,128)S(1)}, f32[256,256]{1,0:T(8,128)S(1)}, u32[]{:S(2)}, u32[]{:S(2)}) %collective-permute-start.4) | collective-permute-done | bytes 262176 | tf_op jit(solution)/shard_map/ppermute | solution.py:137
  145.9 10.6 %shard_map.60 = (f32[256,256]{1,0:T(8,128)S(1)}, f32[256,256]{1,0:T(8,128)S(1)}, f32[256,256]{1,0:T(8,128)S(1)}) custom-call(f32[256,256]{1,0:T(8,128)S(1)} %get-tuple-element.22.refs_0_, f32[256,256]{1,0:T(8,128)S(1)} %get-tuple-element.23.refs_1_, f32[256,256]{1,0:T(8,128)S(1)} %add.56.refs_2_, f32[512,256]{1,0:T(8,128)S(1)} %collective-permute-done.3.refs_3_, ...), custom_call_target="tpu_custom_call" | custom-call | flops 1073741824 | bytes 2097152 | tf_op jit(solution)/shard_map/pallas_call | solution.py:124
  157.5 3.2 %collective-permute-start.6 = (f32[256,256]{1,0:T(8,128)S(1)}, f32[256,256]{1,0:T(8,128)S(1)}, u32[]{:S(2)}, u32[]{:S(2)}) collective-permute-start(f32[256,256]{1,0:T(8,128)S(1)} %add.57.refs_2_), channel_id=1, source_target_pairs={{0,4},{1,5},{2,6},{3,7},{4,0},{5,1},{6,2},{7,3},{8,12},{9,13},{10,... | collective-permute-start | bytes 786440 | tf_op jit(solution)/shard_map/ppermute | solution.py:137
  160.7 16.5 %collective-permute-done.6.refs_4_ = f32[256,256]{1,0:T(8,128)S(1)} collective-permute-done((f32[256,256]{1,0:T(8,128)S(1)}, f32[256,256]{1,0:T(8,128)S(1)}, u32[]{:S(2)}, u32[]{:S(2)}) %collective-permute-start.6) | collective-permute-done | bytes 262176 | tf_op jit(solution)/shard_map/ppermute | solution.py:137
  177.2 10.6 %shard_map.61 = (f32[256,256]{1,0:T(8,128)S(1)}, f32[256,256]{1,0:T(8,128)S(1)}, f32[256,256]{1,0:T(8,128)S(1)}) custom-call(f32[256,256]{1,0:T(8,128)S(1)} %get-tuple-element.25.refs_0_, f32[256,256]{1,0:T(8,128)S(1)} %get-tuple-element.26.refs_1_, f32[256,256]{1,0:T(8,128)S(1)} %add.57.refs_2_, f32[512,256]{1,0:T(8,128)S(1)} %collective-permute-done.5.refs_3_, ...), custom_call_target="tpu_custom_call" | custom-call | flops 1073741824 | bytes 2097152 | tf_op jit(solution)/shard_map/pallas_call | solution.py:124
  188.0 2.3 collective-permute-start.8
  190.2 15.8 %collective-permute-done.8.refs_4_ = f32[256,256]{1,0:T(8,128)S(1)} collective-permute-done((f32[256,256]{1,0:T(8,128)S(1)}, f32[256,256]{1,0:T(8,128)S(1)}, u32[]{:S(2)}, u32[]{:S(2)}) %collective-permute-start.8) | collective-permute-done | bytes 262176 | tf_op jit(solution)/shard_map/ppermute | solution.py:137
  206.1 10.6 %shard_map.62 = (f32[256,256]{1,0:T(8,128)S(1)}, f32[256,256]{1,0:T(8,128)S(1)}, f32[256,256]{1,0:T(8,128)S(1)}) custom-call(f32[256,256]{1,0:T(8,128)S(1)} %get-tuple-element.28.refs_0_, f32[256,256]{1,0:T(8,128)S(1)} %get-tuple-element.29.refs_1_, f32[256,256]{1,0:T(8,128)S(1)} %add.58.refs_2_, f32[512,256]{1,0:T(8,128)S(1)} %collective-permute-done.7.refs_3_, ...), custom_call_target="tpu_custom_call" | custom-call | flops 1073741824 | bytes 2097152 | tf_op jit(solution)/shard_map/pallas_call | solution.py:124
  216.8 3.6 %collective-permute-start.10 = (f32[256,256]{1,0:T(8,128)S(1)}, f32[256,256]{1,0:T(8,128)S(1)}, u32[]{:S(2)}, u32[]{:S(2)}) collective-permute-start(f32[256,256]{1,0:T(8,128)S(1)} %add.59.refs_2_), channel_id=1, source_target_pairs={{0,16},{8,24},{16,0},{24,8},{32,48},{40,56},{48,32},{56,40},{64,80... | collective-permute-start | bytes 786440 | tf_op jit(solution)/shard_map/ppermute | solution.py:137
  220.4 15.1 %collective-permute-done.10.refs_4_ = f32[256,256]{1,0:T(8,128)S(1)} collective-permute-done((f32[256,256]{1,0:T(8,128)S(1)}, f32[256,256]{1,0:T(8,128)S(1)}, u32[]{:S(2)}, u32[]{:S(2)}) %collective-permute-start.10) | collective-permute-done | bytes 262176 | tf_op jit(solution)/shard_map/ppermute | solution.py:137
  235.9 10.6 %shard_map.63 = (f32[256,256]{1,0:T(8,128)S(1)}, f32[256,256]{1,0:T(8,128)S(1)}, f32[256,256]{1,0:T(8,128)S(1)}) custom-call(f32[256,256]{1,0:T(8,128)S(1)} %get-tuple-element.31.refs_0_, f32[256,256]{1,0:T(8,128)S(1)} %get-tuple-element.32.refs_1_, f32[256,256]{1,0:T(8,128)S(1)} %add.59.refs_2_, f32[512,256]{1,0:T(8,128)S(1)} %collective-permute-done.9.refs_3_, ...), custom_call_target="tpu_custom_call" | custom-call | flops 1073741824 | bytes 2097152 | tf_op jit(solution)/shard_map/pallas_call | solution.py:124
  250.0 10.1 %collective-permute-done.11.refs_3_ = f32[512,256]{1,0:T(8,128)S(1)} collective-permute-done((f32[512,256]{1,0:T(8,128)S(1)}, f32[512,256]{1,0:T(8,128)S(1)}, u32[]{:S(2)}, u32[]{:S(2)}) %collective-permute-start.11) | collective-permute-done | bytes 524320 | tf_op jit(solution)/shard_map/ppermute | solution.py:137
  260.1 10.6 %shard_map.64 = (f32[256,256]{1,0:T(8,128)S(1)}, f32[256,256]{1,0:T(8,128)S(1)}, f32[256,256]{1,0:T(8,128)S(1)}) custom-call(f32[256,256]{1,0:T(8,128)S(1)} %get-tuple-element.34.refs_0_, f32[256,256]{1,0:T(8,128)S(1)} %get-tuple-element.35.refs_1_, f32[256,256]{1,0:T(8,128)S(1)} %add.60.refs_2_, f32[512,256]{1,0:T(8,128)S(1)} %collective-permute-done.11.refs_3_, ...), custom_call_target="tpu_custom_call" | custom-call | flops 1073741824 | bytes 2097152 | tf_op jit(solution)/shard_map/pallas_call | solution.py:124
  270.7 2.3 collective-permute-start.13
  273.2 8.6 %collective-permute-done.13 = f32[512,256]{1,0:T(8,128)S(1)} collective-permute-done((f32[512,256]{1,0:T(8,128)S(1)}, f32[512,256]{1,0:T(8,128)S(1)}, u32[]{:S(2)}, u32[]{:S(2)}) %collective-permute-start.13) | collective-permute-done | bytes 524320 | tf_op jit(solution)/shard_map/ppermute | solution.py:137
  281.8 11.0 %shard_map.65 = (f32[6,256,256]{2,1,0:T(8,128)S(1)}, f32[256,256]{1,0:T(8,128)}, f32[256,256]{1,0:T(8,128)}) fusion(f32[6,256,256]{2,1,0:T(8,128)S(1)} %bitcast_dynamic-update-slice_fusion.1, f32[256,256]{1,0:T(8,128)S(1)} %get-tuple-element.37, f32[256,256]{1,0:T(8,128)S(1)} %get-tuple-element.38, f32[256,256]{1,0:T(8,128)S(1)} %add.61, ...), kind=kCustom, calls=%fused_computation.9 | custom fusion | flops 1073741824 | bytes 2359296 | tf_op jit(solution)/shard_map/pallas_call | solution.py:124
  (52 shorter events, 15.3 us)
Async XLA Ops:
  7.2 50.7 %all-gather.2.cloned.1.call-start = ((), (), s32[]{:S(2)}) async-start(), calls=%async_computation.1 | async-start | bytes 2228224 | tf_op jit(solution)/shard_map/all_gather | solution.py:146
  7.9 101.0 %reduce-scatter.2.cloned.1.call-start = ((), (), s32[]{:S(2)}) async-start(), calls=%async_computation.2 | async-start | bytes 2359296 | tf_op jit(solution)/shard_map/reduce_scatter | solution.py:152
  75.6 0.9 copy-start.2
  75.6 34.4 %copy-start = (f32[256,256]{1,0:T(8,128)S(1)}, f32[256,256]{1,0:T(8,128)}, u32[]{:S(2)}) copy-start(f32[256,256]{1,0:T(8,128)} %refs_2_.1) | copy-start | bytes 786436
  76.5 9.9 %collective-permute-start = (bf16[256,256]{1,0:T(8,128)(2,1)S(1)}, bf16[256,256]{1,0:T(8,128)(2,1)S(1)}, u32[]{:S(2)}, u32[]{:S(2)}) collective-permute-start(bf16[256,256]{1,0:T(8,128)(2,1)S(1)} %copy-done.2), channel_id=1, source_target_pairs={{0,0},{8,1},{16,2},{24,3},{32,4},{40,5},{48,6},{56,7},{64,8},{72,9... | collective-permute-start | bytes 393224 | tf_op jit(solution)/shard_map/ppermute | solution.py:143
  109.9 2.4 collective-permute-start.1
  110.0 2.3 collective-permute-start.2
  112.3 1.0 copy-start.1
  124.2 21.7 %collective-permute-start.3 = (f32[512,256]{1,0:T(8,128)S(1)}, f32[512,256]{1,0:T(8,128)S(1)}, u32[]{:S(2)}, u32[]{:S(2)}) collective-permute-start(f32[512,256]{1,0:T(8,128)S(1)} %pad_maximum_fusion.1), channel_id=1, source_target_pairs={{0,2},{1,3},{2,0},{3,1},{4,6},{5,7},{6,4},{7,5},{8,10},{9,11},{10,... | collective-permute-start | bytes 1572872 | tf_op jit(solution)/shard_map/ppermute | solution.py:137
  128.1 17.8 %collective-permute-start.4 = (f32[256,256]{1,0:T(8,128)S(1)}, f32[256,256]{1,0:T(8,128)S(1)}, u32[]{:S(2)}, u32[]{:S(2)}) collective-permute-start(f32[256,256]{1,0:T(8,128)S(1)} %add.56.refs_2_), channel_id=1, source_target_pairs={{0,2},{1,3},{2,0},{3,1},{4,6},{5,7},{6,4},{7,5},{8,10},{9,11},{10,... | collective-permute-start | bytes 786440 | tf_op jit(solution)/shard_map/ppermute | solution.py:137
  156.5 20.6 %collective-permute-start.5 = (f32[512,256]{1,0:T(8,128)S(1)}, f32[512,256]{1,0:T(8,128)S(1)}, u32[]{:S(2)}, u32[]{:S(2)}) collective-permute-start(f32[512,256]{1,0:T(8,128)S(1)} %pad_maximum_fusion.2), channel_id=1, source_target_pairs={{0,4},{1,5},{2,6},{3,7},{4,0},{5,1},{6,2},{7,3},{8,12},{9,13},{10,... | collective-permute-start | bytes 1572872 | tf_op jit(solution)/shard_map/ppermute | solution.py:137
  157.5 19.7 %collective-permute-start.6 = (f32[256,256]{1,0:T(8,128)S(1)}, f32[256,256]{1,0:T(8,128)S(1)}, u32[]{:S(2)}, u32[]{:S(2)}) collective-permute-start(f32[256,256]{1,0:T(8,128)S(1)} %add.57.refs_2_), channel_id=1, source_target_pairs={{0,4},{1,5},{2,6},{3,7},{4,0},{5,1},{6,2},{7,3},{8,12},{9,13},{10,... | collective-permute-start | bytes 786440 | tf_op jit(solution)/shard_map/ppermute | solution.py:137
  187.8 18.2 %collective-permute-start.7 = (f32[512,256]{1,0:T(8,128)S(1)}, f32[512,256]{1,0:T(8,128)S(1)}, u32[]{:S(2)}, u32[]{:S(2)}) collective-permute-start(f32[512,256]{1,0:T(8,128)S(1)} %pad_maximum_fusion.3), channel_id=1, source_target_pairs={{0,8},{8,0},{16,24},{24,16},{32,40},{40,32},{48,56},{56,48},{64,72... | collective-permute-start | bytes 1572872 | tf_op jit(solution)/shard_map/ppermute | solution.py:137
  188.0 18.1 %collective-permute-start.8 = (f32[256,256]{1,0:T(8,128)S(1)}, f32[256,256]{1,0:T(8,128)S(1)}, u32[]{:S(2)}, u32[]{:S(2)}) collective-permute-start(f32[256,256]{1,0:T(8,128)S(1)} %add.58.refs_2_), channel_id=1, source_target_pairs={{0,8},{8,0},{16,24},{24,16},{32,40},{40,32},{48,56},{56,48},{64,72... | collective-permute-start | bytes 786440 | tf_op jit(solution)/shard_map/ppermute | solution.py:137
  216.7 19.2 %collective-permute-start.9 = (f32[512,256]{1,0:T(8,128)S(1)}, f32[512,256]{1,0:T(8,128)S(1)}, u32[]{:S(2)}, u32[]{:S(2)}) collective-permute-start(f32[512,256]{1,0:T(8,128)S(1)} %pad_maximum_fusion.4), channel_id=1, source_target_pairs={{0,16},{8,24},{16,0},{24,8},{32,48},{40,56},{48,32},{56,40},{64,80... | collective-permute-start | bytes 1572872 | tf_op jit(solution)/shard_map/ppermute | solution.py:137
  216.8 18.7 %collective-permute-start.10 = (f32[256,256]{1,0:T(8,128)S(1)}, f32[256,256]{1,0:T(8,128)S(1)}, u32[]{:S(2)}, u32[]{:S(2)}) collective-permute-start(f32[256,256]{1,0:T(8,128)S(1)} %add.59.refs_2_), channel_id=1, source_target_pairs={{0,16},{8,24},{16,0},{24,8},{32,48},{40,56},{48,32},{56,40},{64,80... | collective-permute-start | bytes 786440 | tf_op jit(solution)/shard_map/ppermute | solution.py:137
  235.5 13.0 %collective-permute-start.12 = (f32[256,256]{1,0:T(8,128)S(1)}, f32[256,256]{1,0:T(8,128)S(1)}, u32[]{:S(2)}, u32[]{:S(2)}) collective-permute-start(f32[256,256]{1,0:T(8,128)S(1)} %add.60.refs_2_), channel_id=1, source_target_pairs={{0,32},{8,40},{16,48},{24,56},{32,0},{40,8},{48,16},{56,24},{64,96... | collective-permute-start | bytes 786440 | tf_op jit(solution)/shard_map/ppermute | solution.py:137
  246.5 13.6 %collective-permute-start.11 = (f32[512,256]{1,0:T(8,128)S(1)}, f32[512,256]{1,0:T(8,128)S(1)}, u32[]{:S(2)}, u32[]{:S(2)}) collective-permute-start(f32[512,256]{1,0:T(8,128)S(1)} %pad_maximum_fusion.5), channel_id=1, source_target_pairs={{0,32},{8,40},{16,48},{24,56},{32,0},{40,8},{48,16},{56,24},{64,96... | collective-permute-start | bytes 1572872 | tf_op jit(solution)/shard_map/ppermute | solution.py:137
  248.6 24.5 %collective-permute-start.14 = (f32[256,256]{1,0:T(8,128)S(1)}, f32[256,256]{1,0:T(8,128)S(1)}, u32[]{:S(2)}, u32[]{:S(2)}) collective-permute-start(f32[256,256]{1,0:T(8,128)S(1)} %add.61), channel_id=1, source_target_pairs={{0,64},{8,72},{16,80},{24,88},{32,96},{40,104},{48,112},{56,120},{... | collective-permute-start | bytes 786440 | tf_op jit(solution)/shard_map/ppermute | solution.py:137
  270.7 11.1 %collective-permute-start.13 = (f32[512,256]{1,0:T(8,128)S(1)}, f32[512,256]{1,0:T(8,128)S(1)}, u32[]{:S(2)}, u32[]{:S(2)}) collective-permute-start(f32[512,256]{1,0:T(8,128)S(1)} %pad_maximum_fusion.6), channel_id=1, source_target_pairs={{0,64},{8,72},{16,80},{24,88},{32,96},{40,104},{48,112},{56,120},{... | collective-permute-start | bytes 1572872 | tf_op jit(solution)/shard_map/ppermute | solution.py:137
  292.8 1.1 copy-start.3
Sparse Core Ops, SparseCore 0:
  10.1 47.6 all-gather.1
  75.8 33.1 reduce-scatter.1

commit v2 on v1

v2 whole, which is shorter than its diff:
```python
import jax
import jax.numpy as jnp
from jax import lax
from jax.experimental import pallas as pl
from jax.experimental.pallas import tpu as pltpu
from jax.sharding import PartitionSpec as P

MESH = pl.DeviceIdType.MESH
F32=jnp.float32; BF=jnp.bfloat16

def split(x):
    h=x.astype(BF); l=(x-h.astype(F32)).astype(BF); return h,l
def dg(a,b,dims):
    return lax.dot_general(a,b,(dims,((),())),preferred_element_type=F32)
NN=((1,),(0,)); NT=((1,),(1,)); TN=((0,),(0,))
def dot3(a,b,dims=NN):
    ah,al=a if isinstance(a,tuple) else split(a)
    bh,bl=b if isinstance(b,tuple) else split(b)
    return dg(ah,bh,dims)+(dg(ah,bl,dims)+dg(al,bh,dims))

def lanes(v,c): return jnp.broadcast_to(v[:,c:c+1],(8,128))
def subs(v,i): return jnp.broadcast_to(v[i:i+1,:],(8,128))

def factor64(E,off):
    sub=lax.broadcasted_iota(jnp.int32,(8,128),0)
    E=list(E); X=[]
    for p in range(8):
        row=[subs(E[p],i) for i in range(8)]
        a={}
        for i in range(8):
            for j in range(i,8):
                a[i,j]=lanes(row[i],off+8*p+j)
        V={}
        for n in range(p+1,8):
            V[n]=[lanes(E[n],off+8*p+k) for k in range(8)]
        out=[None]*8
        for m in range(4):
            P,Q=2*m,2*m+1
            aa,bb,cc=a[P,P],a[P,Q],a[Q,Q]
            det=aa*cc-bb*bb
            r=1.0/det
            ra=cc*r; rb=bb*r; rc=aa*r
            yp=ra*row[P]-rb*row[Q]
            yq=rc*row[Q]-rb*row[P]
            t={}
            for i in range(Q+1,8):
                u,v=a[P,i],a[Q,i]
                tp=(cc*u-bb*v)*r
                tq=(aa*v-bb*u)*r
                t[i]=(tp,tq)
                for j in range(i,8):
                    a[i,j]=a[i,j]-(tp*a[P,j]+tq*a[Q,j])
                row[i]=row[i]-(tp*row[P]+tq*row[Q])
            for n in range(p+1,8):
                vp,vq=V[n][P],V[n][Q]
                for i in range(Q+1,8):
                    tp,tq=t[i]
                    V[n][i]=V[n][i]-(tp*vp+tq*vq)
                E[n]=E[n]-(vp*yp+vq*yq)
            sp=lax.rsqrt(aa)
            ba=bb/aa
            sq=lax.rsqrt(cc-bb*ba)
            out[P]=sp*row[P]
            out[Q]=sq*(row[Q]-ba*row[P])
        x=out[0]
        for i in range(1,8): x=jnp.where(sub==i,out[i],x)
        X.append(x)
    return X


def eliminate(T, after_block):
    lane = lax.broadcasted_iota(jnp.int32, (8, 128), 1)
    sub = lax.broadcasted_iota(jnp.int32, (8, 128), 0)
    for k in range(4):
        r0 = 64 * k
        off = r0 % 128
        g0 = r0 - off
        E = []
        for p in range(8):
            v = T[r0 + 8 * p : r0 + 8 * p + 8, g0 : g0 + 128]
            inside = (lane >= off) & (lane < off + 64)
            eye = (lane == (64 - off) + 8 * p + sub).astype(F32)
            E.append(jnp.where(inside, v, eye))
        X = jnp.concatenate(factor64(E, off), 0)
        inv = split(X[:, 64 - off : 128 - off])
        block = T[r0 : r0 + 64, :]
        if k < 3:
            Z = dot3(T[r0 + 64 : 256, r0 : r0 + 64], inv, NT)
        Xk = dot3(inv, block)
        rows = lax.broadcasted_iota(jnp.int32, (64, 256), 0) + r0
        columns = lax.broadcasted_iota(jnp.int32, (64, 256), 1)
        T[r0 : r0 + 64, 0:256] = jnp.where(columns >= rows, Xk[:, 0:256], 0.0)
        T[r0 : r0 + 64, 256:512] = Xk[:, 256:512]
        T[r0 : r0 + 64, 512:768] = jnp.where(columns <= rows, Xk[:, 512:768], 0.0)
        after_block(k)
        if k < 3:
            T[r0 + 64 : 256, :] = T[r0 + 64 : 256, :] - dot3(Z, Xk)


def by_level(level, values):
    out = values[-1]
    for i in range(len(values) - 2, -1, -1):
        out = jnp.where(level == i, values[i], out)
    return out


def tree_kernel(s_ref, w_ref, p_ref, leaf_ref, upper_ref, T, recv, p_own, p_oth,
                send_sem, recv_sem, corner_sem, p_send, p_recv):
    me = lax.axis_index("row") * 8 + lax.axis_index("col")

    def partner(level):
        if isinstance(level, int):
            h = 2**level
        else:
            h = by_level(level, [1, 2, 4, 8, 16, 32, 64])
        other = me + h * (1 - 2 * ((me // h) % 2))
        return (other // 8, other % 8)

    def state_copy(level, k):
        c0 = 0 if k < 2 else 128
        return pltpu.make_async_remote_copy(
            src_ref=T.at[64 * k : 64 * k + 64, c0:512],
            dst_ref=recv.at[level, 64 * k : 64 * k + 64, c0:512],
            send_sem=send_sem.at[k],
            recv_sem=recv_sem.at[level, k],
            device_id=partner(level),
            device_id_type=MESH,
        )

    def p_copy(level):
        return pltpu.make_async_remote_copy(
            src_ref=p_own.at[level],
            dst_ref=p_oth.at[level],
            send_sem=p_send.at[level],
            recv_sem=p_recv.at[level],
            device_id=partner(level),
            device_id_type=MESH,
        )

    barrier = pltpu.get_barrier_semaphore()
    for level in range(7):
        pl.semaphore_signal(barrier, inc=1, device_id=partner(level), device_id_type=MESH)
    T[:, 0:256] = s_ref[...]
    T[:, 256:512] = w_ref[...].astype(F32)
    p_own[0] = p_ref[...]
    for level in range(1, 7):
        recv[level, 128:256, 0:128] = jnp.zeros((128, 128), F32)
    pl.semaphore_wait(barrier, 7)
    corner = pltpu.make_async_remote_copy(
        src_ref=T.at[128:256, 0:128],
        dst_ref=recv.at[0, 128:256, 0:128],
        send_sem=corner_sem.at[0],
        recv_sem=corner_sem.at[1],
        device_id=partner(0),
        device_id_type=MESH,
    )
    for k in range(4):
        state_copy(0, k).start()
    corner.start()
    p_copy(0).start()
    corner.wait()
    p_copy(0).wait()
    p_own[1] = p_own[0] + p_oth[0]
    p_copy(1).start()

    rows = lax.broadcasted_iota(jnp.int32, (256, 256), 0)
    columns = lax.broadcasted_iota(jnp.int32, (256, 256), 1)
    eye = rows == columns

    def level_body(level, carry):
        factor = by_level(level, [0.0] + [2.0 ** (-l / 2.0) for l in range(1, 7)])
        for k in range(4):
            state_copy(level, k).wait()
        s, w = T[:, 0:256], T[:, 256:512]
        so, wo = recv[level, :, 0:256], recv[level, :, 256:512]
        s = s - factor * dot3(p_own[level], wo)
        so = so - factor * dot3(p_oth[level], w)
        M = jnp.concatenate([s, so], axis=0)
        mt = split(M.T)
        gram = dot3(mt, M)
        cross = dot3(mt, jnp.concatenate([w, wo], axis=0))
        trace = jnp.sum(jnp.where(eye, gram, 0.0))
        shift = 0.001 * (trace / 256.0 + 1e-6)
        T[:, 0:256] = gram + jnp.where(eye, shift, 0.0)
        T[:, 256:512] = cross
        T[:, 512:768] = jnp.where(eye, 1.0, 0.0)

        def after_block(k):
            @pl.when(level < 6)
            def _():
                state_copy(level + 1, k).start()

            if k == 1:

                @pl.when(level < 6)
                def _():
                    p_copy(level + 1).wait()

                @pl.when(level < 5)
                def _():
                    p_own[level + 2] = p_own[level + 1] + p_oth[level + 1]
                    p_copy(level + 2).start()

        eliminate(T, after_block)
        q = dot3(s, T[:, 512:768], NT)

        @pl.when(level == 0)
        def _():
            leaf_ref[...] = q

        @pl.when(level > 0)
        def _():
            upper_ref[level - 1] = q

        return carry

    lax.fori_loop(0, 7, level_body, 0)


def tree(sample, leaf_probe, coupling):
    vmem = pl.BlockSpec(memory_space=pltpu.VMEM)
    return pl.pallas_call(
        tree_kernel,
        out_shape=[
            jax.ShapeDtypeStruct((256, 256), F32),
            jax.ShapeDtypeStruct((6, 256, 256), F32),
        ],
        in_specs=[vmem] * 3,
        out_specs=[vmem] * 2,
        scratch_shapes=[
            pltpu.VMEM((256, 768), F32),
            pltpu.VMEM((7, 256, 512), F32),
            pltpu.VMEM((7, 256, 256), F32),
            pltpu.VMEM((7, 256, 256), F32),
            pltpu.SemaphoreType.DMA((4,)),
            pltpu.SemaphoreType.DMA((7, 4)),
            pltpu.SemaphoreType.DMA((2,)),
            pltpu.SemaphoreType.DMA((7,)),
            pltpu.SemaphoreType.DMA((7,)),
        ],
        compiler_params=pltpu.CompilerParams(
            collective_id=1, has_side_effects=True, vmem_limit_bytes=40 << 20
        ),
        cost_estimate=pl.CostEstimate(flops=7 << 30, bytes_accessed=7 << 21, transcendentals=0),
    )(sample, leaf_probe, coupling)


def shards(front, tile_mask, probes, coupling):
    row_index = lax.axis_index("row")
    col_index = lax.axis_index("col")
    leaf_probe = lax.ppermute(
        probes, ("row", "col"), [((d % 16) * 8 + d // 16, d) for d in range(128)]
    )
    probe_block = lax.all_gather(probes, "row", axis=0, tiled=True)
    tile_above = row_index * 8 + jnp.arange(8, dtype=jnp.int32)
    tile_across = col_index * 16 + jnp.arange(16, dtype=jnp.int32)
    keep = tile_mask * (tile_above[:, None] // 2 != tile_across[None, :] // 2).astype(jnp.int32)
    masked = front.reshape(8, 256, 16, 256) * keep.astype(BF)[:, None, :, None]
    partial = jnp.dot(masked.reshape(front.shape), probe_block, preferred_element_type=F32)
    sample = lax.psum_scatter(partial, "col", scatter_dimension=0, tiled=True)
    leaf, upper = tree(sample, leaf_probe, coupling)
    return leaf, upper


def solution(mesh):
    in_specs = (P("row", "col"), P("row", "col"), P(("col", "row"), None), P(("row", "col"), None))
    out_specs = (P(("row", "col"), None), P(None, ("row", "col"), None))
    return jax.shard_map(shards, mesh=mesh, in_specs=in_specs, out_specs=out_specs, check_vma=False)
```

time: 307 us -> 245 us (0.80); the launches traced: 301 us -> 244 us
  waiting for transfers between devices: 152 us -> 66.5 us
  Pallas kernels: 63.8 us -> 127 us
  starting transfers between devices: 24.4 us -> 3.35 us
  other arithmetic: 13.2 us -> 0.78 us
    ppermute x14 -> x0, waiting for transfers between devices: 85.2 us -> none  [exchange(): return lax.ppermute(value, axis, [(i, i ^ 1 << bit) for i in range(count)])]
    pallas_call x6 -> x1, Pallas kernels: 63.8 us -> 127 us  [tree(): pl.pallas_call(tree_kernel, out_shape=[jax.ShapeDtypeStruct((256, 256), F...]
    ppermute x14 -> x0, starting transfers between devices: 21.2 us -> none  [exchange(): return lax.ppermute(value, axis, [(i, i ^ 1 << bit) for i in range(count)])]
    pallas_call x1 -> x0, other arithmetic: 11 us -> none  [level_step(): pl.pallas_call(lambda *refs: level_kernel(factor, *refs), out_shape=[squa...]
    unnamed x14 -> x9, local copies, waits for them, and re-layouts: 13.8 us -> 13.4 us
  transfers between devices with their start and end apart: 17 -> 3, of which waited for: 10 -> 3; matrix products, arithmetic and copies ran while one was open for 5% -> 5% of each run, Pallas kernels for 7% -> 0%
where the time goes in v2:
time: 245 us; the launch traced here: 244 us
  Pallas kernels  127 us (52%)
  waiting for transfers between devices  66.5 us (27%)
  matrix products  17.8 us (7%)
  local copies, waits for them, and re-layouts  15.2 us (6%)
  between operations  14.1 us (6%)
  starting transfers between devices  3.35 us (1%)
    pallas_call x1, Pallas kernels, tree(): pl.pallas_call(tree_kernel, out_shape=[jax.ShapeDtypeStruct((256, 256), F...  127 us
    all_gather x1, waiting for transfers between devices, shards(): probe_block = lax.all_gather(probes, 'row', axis=0, tiled=True)  36.7 us
    reduce_scatter x1, waiting for transfers between devices, shards(): sample = lax.psum_scatter(partial, 'col', scatter_dimension=0, tiled=True)  22.5 us
    dot_general x1, matrix products, shards(): jnp.dot(masked.reshape(front.shape), probe_block, preferred_element_type=...  17.8 us
    unnamed x9, local copies, waits for them, and re-layouts  13.4 us
    ppermute x1, waiting for transfers between devices, shards(): lax.ppermute(probes, ('row', 'col'), [(d % 16 * 8 + d // 16, d) for d in...  6.63 us
  transfers between devices with their start and end apart: 3, of which 3 were waited for; matrix products, arithmetic and copies ran while one was open for 5% of the time, Pallas kernels for 0%

profile of v2, /device:TPU:2, one launch (start us, length us, event | category | flops | bytes accessed | tf_op | source)
XLA Modules:
  0.0 244.3 jit_solution(2113047048874118561)
XLA Ops:
  7.2 0.0 all-gather.2.cloned.1.call-start
  7.2 0.7 all-gather.2.cloned.1.call-update
  7.9 0.0 reduce-scatter.2.cloned.1.call-start
  8.0 0.8 select_convert_fusion
  8.7 1.7 mul.23
  10.5 10.6 %copy.6 = bf16[256,8,16,256]{3,1,2,0:T(8,128)(2,1)} copy(bf16[256,8,16,256]{3,2,1,0:T(8,128)(2,1)S(1)} %bitcast.4) | data formatting | bytes 33554432
  21.1 36.7 %all-gather.2.cloned.1.call-done = bf16[4096,256]{1,0:T(8,128)(2,1)} async-done(((bf16[256,256]{1,0:T(8,128)(2,1)}), bf16[4096,256]{1,0:T(8,128)(2,1)}) %all-gather.2.cloned.1.call-update) | async-done | bytes 2097168 | tf_op jit(solution)/shard_map/all_gather | solution.py:254
  57.8 0.0 copy-start.2
  57.8 0.0 copy-start
  57.8 17.8 %fusion = f32[2048,256]{1,0:T(8,128)} fusion(bf16[4096,256]{1,0:T(8,128)(2,1)} %all-gather.2.cloned.1.call-done, bf16[2048,4096]{1,0:T(8,128)(2,1)} %param.4, bf16[2048,4096]{1,0:T(8,128)(2,1)} %bitcast.5), kind=kOutput, calls=%fused_computation | convolution fusion | flops 4303355904 | bytes 37748736 | tf_op jit(solution)/shard_map/dot_general | solution.py:259
  75.7 0.0 reduce-scatter.2.cloned.1.call-update
  75.7 0.0 copy-done.2
  75.7 3.3 %collective-permute-start = (bf16[256,256]{1,0:T(8,128)(2,1)S(1)}, bf16[256,256]{1,0:T(8,128)(2,1)S(1)}, u32[]{:S(2)}, u32[]{:S(2)}) collective-permute-start(bf16[256,256]{1,0:T(8,128)(2,1)S(1)} %copy-done.2), channel_id=1, source_target_pairs={{0,0},{8,1},{16,2},{24,3},{32,4},{40,5},{48,6},{56,7},{64,8},{72,9... | collective-permute-start | bytes 393224 | tf_op jit(solution)/shard_map/ppermute | solution.py:251
  79.0 6.6 %collective-permute-done.w_ref = bf16[256,256]{1,0:T(8,128)(2,1)S(1)} collective-permute-done((bf16[256,256]{1,0:T(8,128)(2,1)S(1)}, bf16[256,256]{1,0:T(8,128)(2,1)S(1)}, u32[]{:S(2)}, u32[]{:S(2)}) %collective-permute-start) | collective-permute-done | bytes 131104 | tf_op jit(solution)/shard_map/ppermute | solution.py:251
  85.6 22.5 %reduce-scatter.2.cloned.1.call-done.s_ref = f32[256,256]{1,0:T(8,128)} async-done(((f32[2048,256]{1,0:T(8,128)}), f32[256,256]{1,0:T(8,128)}) %reduce-scatter.2.cloned.1.call-update) | async-done | bytes 262160 | tf_op jit(solution)/shard_map/reduce_scatter | solution.py:260
  108.1 0.0 copy-done
  108.1 0.0 copy-start.1
  108.1 0.9 copy-done.1
  109.1 126.5 %shard_map.59 = (f32[256,256]{1,0:T(8,128)S(1)}, f32[6,256,256]{2,1,0:T(8,128)S(1)}) custom-call(f32[256,256]{1,0:T(8,128)S(1)} %copy-done.1, bf16[256,256]{1,0:T(8,128)(2,1)S(1)} %collective-permute-done.w_ref, f32[256,256]{1,0:T(8,128)S(1)} %copy-done), custom_call_target="tpu_custom_call" | custom-call | flops 7516192768 | bytes 14680064 | tf_op jit(solution)/shard_map/pallas_call | solution.py:222
  235.6 0.7 copy.9
  236.3 1.1 copy.10
  (2 shorter events, 0.0 us)
Async XLA Ops:
  7.2 50.7 %all-gather.2.cloned.1.call-start = ((), (), s32[]{:S(2)}) async-start(), calls=%async_computation.1 | async-start | bytes 2228224 | tf_op jit(solution)/shard_map/all_gather | solution.py:254
  7.9 100.2 %reduce-scatter.2.cloned.1.call-start = ((), (), s32[]{:S(2)}) async-start(), calls=%async_computation.2 | async-start | bytes 2359296 | tf_op jit(solution)/shard_map/reduce_scatter | solution.py:260
  57.8 17.9 %copy-start.2 = (bf16[256,256]{1,0:T(8,128)(2,1)S(1)}, bf16[256,256]{1,0:T(8,128)(2,1)}, u32[]{:S(2)}) copy-start(bf16[256,256]{1,0:T(8,128)(2,1)} %param.6) | copy-start | bytes 393220
  57.8 50.3 %copy-start = (f32[256,256]{1,0:T(8,128)S(1)}, f32[256,256]{1,0:T(8,128)}, u32[]{:S(2)}) copy-start(f32[256,256]{1,0:T(8,128)} %p_ref.1) | copy-start | bytes 786436
  75.7 9.9 %collective-permute-start = (bf16[256,256]{1,0:T(8,128)(2,1)S(1)}, bf16[256,256]{1,0:T(8,128)(2,1)S(1)}, u32[]{:S(2)}, u32[]{:S(2)}) collective-permute-start(bf16[256,256]{1,0:T(8,128)(2,1)S(1)} %copy-done.2), channel_id=1, source_target_pairs={{0,0},{8,1},{16,2},{24,3},{32,4},{40,5},{48,6},{56,7},{64,8},{72,9... | collective-permute-start | bytes 393224 | tf_op jit(solution)/shard_map/ppermute | solution.py:251
  108.1 1.0 copy-start.1
Sparse Core Ops, SparseCore 0:
  10.1 47.6 all-gather.1
  75.8 32.2 reduce-scatter.1

commit v3 on v2

--- a/solution.py
+++ b/solution.py
@@ -245,19 +245,200 @@
     )(sample, leaf_probe, coupling)
 
 
+def front_kernel(front_ref, keep_ref, probes_ref, s_ref, w_ref, F, B, acc, from_core, from_x, leaf,
+                 f_sem, near_send, near_recv, far_send, far_recv, c_send, c_recv, x_send, x_recv, l_sem):
+    row, col = lax.axis_index("row"), lax.axis_index("col")
+    z, y = row // 4, row % 4
+    x, c = col // 2, col % 2
+    me = row * 8 + col
+    target = col * 16 + row
+    source = (me % 16, me // 16)
+    moved = target != me
+
+    def at(dz, dy):
+        return ((z + dz + 4) % 4 * 4 + (y + dy + 4) % 4, col)
+
+    def along_x(d, other):
+        core = 1 - c if other else c
+        return (row, (x + d) % 4 * 2 + core)
+
+    def half_rows(dz, dy, h):
+        block = (z + dz + 4) % 4 * 4 + (y + dy + 4) % 4
+        return pl.ds(pl.multiple_of(block * 256 + h * 128, 128), 128)
+
+    def columns_of(d):
+        return pl.ds(pl.multiple_of((z + 4 - d) % 4 * 1024, 1024), 1024)
+
+    def remote(src, dst, send, recv, device):
+        return pltpu.make_async_remote_copy(
+            src_ref=src, dst_ref=dst, send_sem=send, recv_sem=recv, device_id=device, device_id_type=MESH
+        )
+
+    def load(d):
+        return pltpu.make_async_copy(front_ref.at[:, columns_of(d)], F.at[:, columns_of(d)], f_sem.at[d])
+
+    def near(h, d):
+        r = half_rows(0, 0, h)
+        return remote(B.at[r], B.at[r], near_send.at[h, d - 1], near_recv.at[h, d - 1],
+                      at(0, d) if h == 0 else at(d, 0))
+
+    def far(h, held, d):
+        r = half_rows(0, -held, 0) if h == 0 else half_rows(-held, 0, 1)
+        return remote(B.at[r], B.at[r], far_send.at[h, held, d - 1], far_recv.at[h, held, d - 1],
+                      at(d, 0) if h == 0 else at(0, d))
+
+    def to_core(d):
+        t = pl.ds(pl.multiple_of(((x + d) % 4 * 2 + 1 - c) * 256, 256), 256)
+        return remote(acc.at[t], from_core.at[d], c_send.at[d], c_recv.at[d], along_x(0, True))
+
+    def to_x(d):
+        t = pl.ds(pl.multiple_of(((x + d) % 4 * 2 + c) * 256, 256), 256)
+        return remote(acc.at[t], from_x.at[d - 1], x_send.at[d - 1], x_recv.at[d - 1], along_x(d, False))
+
+    def to_leaf():
+        return remote(probes_ref, leaf, l_sem.at[0], l_sem.at[1], (target // 8, target % 8))
+
+    order = (0, 1, 3, 2)
+    for d in order:
+        load(d).start()
+    barrier = pltpu.get_barrier_semaphore()
+    peers = [at(d, 0) for d in (1, 2, 3)] + [at(0, d) for d in (1, 2, 3)]
+    peers += [along_x(d, False) for d in (1, 2, 3)] + [along_x(0, True)]
+    for peer in peers:
+        pl.semaphore_signal(barrier, inc=1, device_id=peer, device_id_type=MESH)
+    pl.semaphore_signal(barrier, inc=1, device_id=source, device_id_type=MESH)
+
+    own = pl.ds(pl.multiple_of(row * 256, 256), 256)
+    B[own, :] = probes_ref[...]
+    pl.semaphore_wait(barrier, 11)
+
+    for d in (1, 3, 2):
+        near(0, d).start()
+        near(1, d).start()
+    for d in (1, 3, 2):
+        far(0, 0, d).start()
+        far(1, 0, d).start()
+    for held in (1, 3, 2):
+        near(0, held).wait_recv()
+        near(1, held).wait_recv()
+        for d in (1, 3, 2):
+            far(0, held, d).start()
+            far(1, held, d).start()
+
+    @pl.when(moved)
+    def _():
+        to_leaf().start()
+
+    @pl.when(jnp.logical_not(moved))
+    def _():
+        leaf[...] = probes_ref[...]
+
+    def product(a, d):
+        r = pl.ds(pl.multiple_of(a * 256, 256), 256)
+        k = keep_ref[pl.ds(a, 1), columns_of(d)].astype(BF)
+        return jnp.dot(F[r, columns_of(d)] * k, B[columns_of(d), :], preferred_element_type=F32)
+
+    for d in order:
+        load(d).wait()
+        if d == 0:
+            for e in (1, 2, 3):
+                far(1, 0, e).wait_recv()
+        else:
+            for e in range(4):
+                far(0, e, d).wait_recv()
+            for e in (1, 2, 3):
+                far(1, d, e).wait_recv()
+        if d != order[-1]:
+
+            def body(a, carry):
+                r = pl.ds(pl.multiple_of(a * 256, 256), 256)
+                p = product(a, d)
+                acc[r, :] = p if d == 0 else acc[r, :] + p
+                return carry
+
+            lax.fori_loop(0, 8, body, 0)
+
+    def finish(e):
+        to_core(e).wait_recv()
+        r = pl.ds(pl.multiple_of(((x + e) % 4 * 2 + c) * 256, 256), 256)
+        acc[r, :] = acc[r, :] + from_core[e]
+        if e:
+            to_x(e).start()
+
+    ahead = None
+    for e in (2, 1, 3, 0):
+        for other in (True, False):
+            a = (x + e) % 4 * 2 + (1 - c if other else c)
+            r = pl.ds(pl.multiple_of(a * 256, 256), 256)
+            acc[r, :] = acc[r, :] + product(a, order[-1])
+            if other:
+                to_core(e).start()
+        if ahead is not None:
+            finish(ahead)
+        ahead = e
+    finish(0)
+    total = acc[pl.ds(pl.multiple_of(col * 256, 256), 256), :]
+    for d in (1, 3, 2):
+        to_x(d).wait_recv()
+        total = total + from_x[d - 1]
+    s_ref[...] = total
+
+    @pl.when(moved)
+    def _():
+        to_leaf().wait()
+
+    w_ref[...] = leaf[...]
+    for h in (0, 1):
+        for d in (1, 2, 3):
+            near(h, d).wait_send()
+            for held in range(4):
+                far(h, held, d).wait_send()
+    for d in range(4):
+        to_core(d).wait_send()
+    for d in (1, 2, 3):
+        to_x(d).wait_send()
+
+
+def samples(front, keep, probes):
+    vmem = pl.BlockSpec(memory_space=pltpu.VMEM)
+    return pl.pallas_call(
+        front_kernel,
+        out_shape=[jax.ShapeDtypeStruct((256, 256), F32), jax.ShapeDtypeStruct((256, 256), BF)],
+        in_specs=[pl.BlockSpec(memory_space=pl.ANY), vmem, vmem],
+        out_specs=[vmem] * 2,
+        scratch_shapes=[
+            pltpu.VMEM((2048, 4096), BF),
+            pltpu.VMEM((4096, 256), BF),
+            pltpu.VMEM((2048, 256), F32),
+            pltpu.VMEM((4, 256, 256), F32),
+            pltpu.VMEM((3, 256, 256), F32),
+            pltpu.VMEM((256, 256), BF),
+            pltpu.SemaphoreType.DMA((4,)),
+            pltpu.SemaphoreType.DMA((2, 3)),
+            pltpu.SemaphoreType.DMA((2, 3)),
+            pltpu.SemaphoreType.DMA((2, 4, 3)),
+            pltpu.SemaphoreType.DMA((2, 4, 3)),
+            pltpu.SemaphoreType.DMA((4,)),
+            pltpu.SemaphoreType.DMA((4,)),
+            pltpu.SemaphoreType.DMA((3,)),
+            pltpu.SemaphoreType.DMA((3,)),
+            pltpu.SemaphoreType.DMA((2,)),
+        ],
+        compiler_params=pltpu.CompilerParams(
+            collective_id=2, has_side_effects=True, vmem_limit_bytes=44 << 20
+        ),
+        cost_estimate=pl.CostEstimate(flops=1 << 32, bytes_accessed=1 << 24, transcendentals=0),
+    )(front, keep, probes)
+
+
 def shards(front, tile_mask, probes, coupling):
     row_index = lax.axis_index("row")
     col_index = lax.axis_index("col")
-    leaf_probe = lax.ppermute(
-        probes, ("row", "col"), [((d % 16) * 8 + d // 16, d) for d in range(128)]
-    )
-    probe_block = lax.all_gather(probes, "row", axis=0, tiled=True)
     tile_above = row_index * 8 + jnp.arange(8, dtype=jnp.int32)
     tile_across = col_index * 16 + jnp.arange(16, dtype=jnp.int32)
     keep = tile_mask * (tile_above[:, None] // 2 != tile_across[None, :] // 2).astype(jnp.int32)
-    masked = front.reshape(8, 256, 16, 256) * keep.astype(BF)[:, None, :, None]
-    partial = jnp.dot(masked.reshape(front.shape), probe_block, preferred_element_type=F32)
-    sample = lax.psum_scatter(partial, "col", scatter_dimension=0, tiled=True)
+    keep = jnp.repeat(keep.astype(F32), 256, axis=1)
+    sample, leaf_probe = samples(front, keep, probes)
     leaf, upper = tree(sample, leaf_probe, coupling)
     return leaf, upper
 

time: 245 us -> 177 us (0.72)
  waiting for transfers between devices: 66.5 us -> 0 us
  Pallas kernels: 127 us -> 172 us
  matrix products: 17.8 us -> 0 us
  between operations: 14.1 us -> 0.69 us
  local copies, waits for them, and re-layouts: 15.2 us -> 2.9 us
  starting transfers between devices: 3.35 us -> 0 us
    pallas_call x0 -> x1, Pallas kernels: none -> 45 us  [samples(): pl.pallas_call(front_kernel, out_shape=[jax.ShapeDtypeStruct((256, 256),...]
    all_gather x1 -> x0, waiting for transfers between devices: 36.7 us -> none  [shards(): probe_block = lax.all_gather(probes, 'row', axis=0, tiled=True)]
    reduce_scatter x1 -> x0, waiting for transfers between devices: 22.5 us -> none  [shards(): sample = lax.psum_scatter(partial, 'col', scatter_dimension=0, tiled=True)]
    dot_general x1 -> x0, matrix products: 17.8 us -> none  [shards(): jnp.dot(masked.reshape(front.shape), probe_block, preferred_element_type=...]
    unnamed x9 -> x6, local copies, waits for them, and re-layouts: 13.4 us -> 2.75 us
    ppermute x1 -> x0, waiting for transfers between devices: 6.63 us -> none  [shards(): lax.ppermute(probes, ('row', 'col'), [(d % 16 * 8 + d // 16, d) for d in...]
    ppermute x1 -> x0, starting transfers between devices: 3.28 us -> none  [shards(): lax.ppermute(probes, ('row', 'col'), [(d % 16 * 8 + d // 16, d) for d in...]
  transfers between devices with their start and end apart: 3 -> 0, of which waited for: 3 -> 0; matrix products, arithmetic and copies ran while one was open for 5% -> 0% of each run, Pallas kernels for 0% -> 0%
where the time goes in v3:
time: 177 us
  Pallas kernels  172 us (97%)
  local copies, waits for them, and re-layouts  2.9 us (2%)
    pallas_call x1, Pallas kernels, tree(): pl.pallas_call(tree_kernel, out_shape=[jax.ShapeDtypeStruct((256, 256), F...  127 us
    pallas_call x1, Pallas kernels, samples(): pl.pallas_call(front_kernel, out_shape=[jax.ShapeDtypeStruct((256, 256),...  45 us

profile of v3, /device:TPU:2, one launch (start us, length us, event | category | flops | bytes accessed | tf_op | source)
XLA Modules:
  0.0 176.7 jit_solution(18389095730678999583)
XLA Ops:
  0.7 0.8 select_convert_fusion
  1.4 0.1 copy.6
  1.5 0.1 broadcast_in_dim.2
  1.6 0.0 copy-start
  1.6 0.9 copy-done
  2.5 0.0 copy-start.1
  2.5 45.0 %shard_map.59 = (f32[256,256]{1,0:T(8,128)S(1)}, bf16[256,256]{1,0:T(8,128)(2,1)S(1)}) custom-call(bf16[2048,4096]{1,0:T(8,128)(2,1)} %front_ref.1, f32[8,4096]{1,0:T(8,128)S(1)} %bitcast.1, bf16[256,256]{1,0:T(8,128)(2,1)S(1)} %copy-done), custom_call_target="tpu_custom_call" | custom-call | flops 4294967296 | bytes 16777216 | tf_op jit(solution)/shard_map/pallas_call | solution.py:404
  47.5 0.0 copy-done.1
  47.5 127.3 %shard_map.60 = (f32[256,256]{1,0:T(8,128)S(1)}, f32[6,256,256]{2,1,0:T(8,128)S(1)}) custom-call(f32[256,256]{1,0:T(8,128)S(1)} %get-tuple-element.4.s_ref, bf16[256,256]{1,0:T(8,128)(2,1)S(1)} %get-tuple-element.5.w_ref, f32[256,256]{1,0:T(8,128)S(1)} %copy-done.1), custom_call_target="tpu_custom_call" | custom-call | flops 7516192768 | bytes 14680064 | tf_op jit(solution)/shard_map/pallas_call | solution.py:222
  174.9 0.7 copy.9
  175.6 1.1 copy.10
  (2 shorter events, 0.0 us)
Async XLA Ops:
  1.6 0.9 copy-start
  2.5 45.0 %copy-start.1 = (f32[256,256]{1,0:T(8,128)S(1)}, f32[256,256]{1,0:T(8,128)}, u32[]{:S(2)}) copy-start(f32[256,256]{1,0:T(8,128)} %p_ref.1) | copy-start | bytes 786436

commit v4 on v3

v4 whole, which is shorter than its diff:
```python
import jax
import jax.numpy as jnp
from jax import lax
from jax.experimental import pallas as pl
from jax.experimental.pallas import tpu as pltpu
from jax.sharding import PartitionSpec as P

MESH = pl.DeviceIdType.MESH
F32=jnp.float32; BF=jnp.bfloat16

def split(x):
    h=x.astype(BF); l=(x-h.astype(F32)).astype(BF); return h,l
def dg(a,b,dims):
    return lax.dot_general(a,b,(dims,((),())),preferred_element_type=F32)
NN=((1,),(0,)); NT=((1,),(1,)); TN=((0,),(0,))
def dot3(a,b,dims=NN):
    ah,al=a if isinstance(a,tuple) else split(a)
    bh,bl=b if isinstance(b,tuple) else split(b)
    return dg(ah,bh,dims)+(dg(ah,bl,dims)+dg(al,bh,dims))

def lanes(v,c): return jnp.broadcast_to(v[:,c:c+1],(8,128))
def subs(v,i): return jnp.broadcast_to(v[i:i+1,:],(8,128))

def rcp(x):
    return pltpu.reciprocal(x,approx=True)
def factor64(E,off):
    sub=lax.broadcasted_iota(jnp.int32,(8,128),0)
    E=list(E); X=[]
    D=[lanes(E[0],off+j) for j in range(8)]
    for p in range(8):
        V={n:[lanes(E[n],off+8*p+k) for k in range(8)] for n in range(p+1,8)}
        ahead=[lanes(E[p+1],off+8*p+8+j) for j in range(8)] if p<7 else None
        out=None
        for m in range(4):
            P,Q=2*m,2*m+1
            vp,vq=D[P],D[Q]
            aa,bb,cc=subs(vp,P),subs(vq,P),subs(vq,Q)
            r=rcp(aa*cc-bb*bb)
            ep,eq=subs(E[p],P),subs(E[p],Q)
            yp=(cc*ep-bb*eq)*r
            yq=(aa*eq-bb*ep)*r
            zp=(cc*vp-bb*vq)*r
            zq=(aa*vq-bb*vp)*r
            z={j:(subs(zp,j),subs(zq,j)) for j in range(Q+1,8)}
            if m<3:
                mp=jnp.where(sub>Q,vp,0.0); mq=jnp.where(sub>Q,vq,0.0)
                for j in range(Q+1,8):
                    D[j]=D[j]-(mp*z[j][0]+mq*z[j][1])
                E[p]=E[p]-(mp*yp+mq*yq)
            for n in range(p+1,8):
                wp,wq=V[n][P],V[n][Q]
                if n==p+1:
                    tp=(cc*wp-bb*wq)*r
                    tq=(aa*wq-bb*wp)*r
                    for j in range(8):
                        ahead[j]=ahead[j]-(wp*subs(tp,j)+wq*subs(tq,j))
                for j in range(Q+1,8):
                    V[n][j]=V[n][j]-(wp*z[j][0]+wq*z[j][1])
                E[n]=E[n]-(wp*yp+wq*yq)
            ba=bb*rcp(aa)
            sp=lax.rsqrt(aa); sq=lax.rsqrt(cc-bb*ba)
            xp=sp*ep; xq=sq*(eq-ba*ep)
            out=xp if out is None else jnp.where(sub==P,xp,out)
            out=jnp.where(sub==Q,xq,out)
        X.append(out)
        D=ahead
    return X

def eliminate(T, after_block):
    lane = lax.broadcasted_iota(jnp.int32, (8, 128), 1)
    sub = lax.broadcasted_iota(jnp.int32, (8, 128), 0)
    for k in range(4):
        r0 = 64 * k
        off = r0 % 128
        g0 = r0 - off
        E = []
        for p in range(8):
            v = T[r0 + 8 * p : r0 + 8 * p + 8, g0 : g0 + 128]
            inside = (lane >= off) & (lane < off + 64)
            eye = (lane == (64 - off) + 8 * p + sub).astype(F32)
            E.append(jnp.where(inside, v, eye))
        X = jnp.concatenate(factor64(E, off), 0)
        inv = split(X[:, 64 - off : 128 - off])
        block = T[r0 : r0 + 64, :]
        if k < 3:
            Z = dot3(T[r0 + 64 : 256, r0 : r0 + 64], inv, NT)
        Xk = dot3(inv, block)
        rows = lax.broadcasted_iota(jnp.int32, (64, 256), 0) + r0
        columns = lax.broadcasted_iota(jnp.int32, (64, 256), 1)
        T[r0 : r0 + 64, 0:256] = jnp.where(columns >= rows, Xk[:, 0:256], 0.0)
        T[r0 : r0 + 64, 256:512] = Xk[:, 256:512]
        T[r0 : r0 + 64, 512:768] = jnp.where(columns <= rows, Xk[:, 512:768], 0.0)
        after_block(k)
        if k < 3:
            T[r0 + 64 : 256, :] = T[r0 + 64 : 256, :] - dot3(Z, Xk)


def by_level(level, values):
    out = values[-1]
    for i in range(len(values) - 2, -1, -1):
        out = jnp.where(level == i, values[i], out)
    return out


def whole_kernel(front_ref, keep_ref, probes_ref, p_ref, leaf_ref, upper_ref,
                 F, B, acc, from_core, from_x, leaf, T, recv, p_own, p_oth,
                 f_sem, near_send, near_recv, far_send, far_recv, c_send, c_recv, x_send, x_recv, l_sem,
                 d_send, d_recv, w_send, w_recv, p_send, p_recv):
    row, col = lax.axis_index("row"), lax.axis_index("col")
    z, y = row // 4, row % 4
    x, c = col // 2, col % 2
    me = row * 8 + col
    target = col * 16 + row
    source = (me % 16, me // 16)
    moved = target != me

    def at(dz, dy):
        return ((z + dz + 4) % 4 * 4 + (y + dy + 4) % 4, col)

    def along_x(d, other):
        core = 1 - c if other else c
        return (row, (x + d) % 4 * 2 + core)

    def half_rows(dz, dy, h):
        block = (z + dz + 4) % 4 * 4 + (y + dy + 4) % 4
        return pl.ds(pl.multiple_of(block * 256 + h * 128, 128), 128)

    def columns_of(d):
        return pl.ds(pl.multiple_of((z + 4 - d) % 4 * 1024, 1024), 1024)

    def remote(src, dst, send, recv, device):
        return pltpu.make_async_remote_copy(
            src_ref=src, dst_ref=dst, send_sem=send, recv_sem=recv, device_id=device, device_id_type=MESH
        )

    def load(d):
        return pltpu.make_async_copy(front_ref.at[:, columns_of(d)], F.at[:, columns_of(d)], f_sem.at[d])

    def near(h, d):
        r = half_rows(0, 0, h)
        return remote(B.at[r], B.at[r], near_send.at[h, d - 1], near_recv.at[h, d - 1],
                      at(0, d) if h == 0 else at(d, 0))

    def far(h, held, d):
        r = half_rows(0, -held, 0) if h == 0 else half_rows(-held, 0, 1)
        return remote(B.at[r], B.at[r], far_send.at[h, held, d - 1], far_recv.at[h, held, d - 1],
                      at(d, 0) if h == 0 else at(0, d))

    def to_core(d):
        t = pl.ds(pl.multiple_of(((x + d) % 4 * 2 + 1 - c) * 256, 256), 256)
        return remote(acc.at[t], from_core.at[d], c_send.at[d], c_recv.at[d], along_x(0, True))

    def to_x(d):
        t = pl.ds(pl.multiple_of(((x + d) % 4 * 2 + c) * 256, 256), 256)
        return remote(acc.at[t], from_x.at[d - 1], x_send.at[d - 1], x_recv.at[d - 1], along_x(d, False))

    def to_leaf():
        return remote(probes_ref, leaf, l_sem.at[0], l_sem.at[1], (target // 8, target % 8))

    def partner(level):
        h = 2**level if isinstance(level, int) else by_level(level, [1, 2, 4, 8, 16, 32, 64])
        other = me + h * (1 - 2 * ((me // h) % 2))
        return (other // 8, other % 8)

    def p_copy(level):
        return remote(p_own.at[level], p_oth.at[level], p_send.at[level], p_recv.at[level], partner(level))

    def p_step(level):
        p_copy(level).wait()
        p_own[level + 1] = p_own[level] + p_oth[level]

    def part(k, core):
        if k == 3:
            return pl.ds(192, 64), pl.ds(128, 384)
        c0 = 0 if k < 2 else 128
        return pl.ds(pl.multiple_of(64 * k + 32 * core, 32), 32), pl.ds(c0, 512 - c0)

    def direct(level, k):
        r, l = part(k, c)
        return remote(T.at[r, l], recv.at[level, r, l], d_send.at[k], d_recv.at[level, k], partner(level))

    def passed(level, k):
        r, l = part(k, c)
        return remote(recv.at[level, r, l], recv.at[level, r, l], w_send.at[k], w_recv.at[level, k], partner(0))

    order = (0, 1, 3, 2)
    for d in order:
        load(d).start()
    barrier = pltpu.get_barrier_semaphore()
    peers = [at(d, 0) for d in (1, 2, 3)] + [at(0, d) for d in (1, 2, 3)]
    peers += [along_x(d, False) for d in (1, 2, 3)] + [along_x(0, True)]
    for peer in peers:
        pl.semaphore_signal(barrier, inc=1, device_id=peer, device_id_type=MESH)
    pl.semaphore_signal(barrier, inc=1, device_id=source, device_id_type=MESH)

    own = pl.ds(pl.multiple_of(row * 256, 256), 256)
    B[own, :] = probes_ref[...]
    p_own[0] = p_ref[...]
    pl.semaphore_wait(barrier, 11)

    for d in (1, 3, 2):
        near(0, d).start()
        near(1, d).start()
    for d in (1, 3, 2):
        far(0, 0, d).start()
        far(1, 0, d).start()
    p_copy(0).start()
    for held in (1, 3, 2):
        near(0, held).wait_recv()
        near(1, held).wait_recv()
        for d in (1, 3, 2):
            far(0, held, d).start()
            far(1, held, d).start()

    @pl.when(moved)
    def _():
        to_leaf().start()

    @pl.when(jnp.logical_not(moved))
    def _():
        leaf[...] = probes_ref[...]

    p_step(0)
    p_copy(1).start()

    def product(a, d):
        r = pl.ds(pl.multiple_of(a * 256, 256), 256)
        k = keep_ref[pl.ds(a, 1), columns_of(d)].astype(BF)
        return jnp.dot(F[r, columns_of(d)] * k, B[columns_of(d), :], preferred_element_type=F32)

    for d in order:
        load(d).wait()
        if d == 0:
            for e in (1, 2, 3):
                far(1, 0, e).wait_recv()
        else:
            for e in range(4):
                far(0, e, d).wait_recv()
            for e in (1, 2, 3):
                far(1, d, e).wait_recv()
        if d != order[-1]:

            def body(a, carry):
                r = pl.ds(pl.multiple_of(a * 256, 256), 256)
                p = product(a, d)
                acc[r, :] = p if d == 0 else acc[r, :] + p
                return carry

            lax.fori_loop(0, 8, body, 0)
            if d == order[1]:
                p_step(1)
                p_copy(2).start()

    def finish(e):
        to_core(e).wait_recv()
        r = pl.ds(pl.multiple_of(((x + e) % 4 * 2 + c) * 256, 256), 256)
        acc[r, :] = acc[r, :] + from_core[e]
        if e:
            to_x(e).start()

    ahead = None
    for e in (2, 1, 3, 0):
        for other in (True, False):
            a = (x + e) % 4 * 2 + (1 - c if other else c)
            r = pl.ds(pl.multiple_of(a * 256, 256), 256)
            acc[r, :] = acc[r, :] + product(a, order[-1])
            if other:
                to_core(e).start()
        if ahead is not None:
            finish(ahead)
        ahead = e
    finish(0)
    total = acc[pl.ds(pl.multiple_of(col * 256, 256), 256), :]
    for d in (1, 3, 2):
        to_x(d).wait_recv()
        total = total + from_x[d - 1]
    p_step(2)
    T[:, 0:256] = total

    @pl.when(moved)
    def _():
        to_leaf().wait()

    T[:, 256:512] = leaf[...].astype(F32)
    corner = remote(T.at[128:256, 0:128], recv.at[0, 128:256, 0:128], l_sem.at[2], l_sem.at[3], partner(0))
    corner.start()
    for k in range(4):
        direct(0, k).start()
        if k < 3:
            r, l = part(k, 1 - c)
            remote(T.at[r, l], recv.at[0, r, l], w_send.at[k], w_recv.at[0, k], partner(0)).start()
    for level in range(1, 7):
        recv[level, 128:256, 0:128] = jnp.zeros((128, 128), F32)
    for h in (0, 1):
        for d in (1, 2, 3):
            near(h, d).wait_send()
            for held in range(4):
                far(h, held, d).wait_send()
    for d in range(4):
        to_core(d).wait_send()
    for d in (1, 2, 3):
        to_x(d).wait_send()
    corner.wait()
    for k in range(3):
        direct(0, k).wait_recv()

    rows = lax.broadcasted_iota(jnp.int32, (256, 256), 0)
    columns = lax.broadcasted_iota(jnp.int32, (256, 256), 1)
    eye = rows == columns

    def level_body(level, carry):
        factor = by_level(level, [0.0] + [2.0 ** (-l / 2.0) for l in range(1, 7)])

        @pl.when(level == 1)
        def _():
            p_step(4)

        @pl.when(level == 2)
        def _():
            p_copy(6).wait()

        @pl.when(level < 2)
        def _():
            p_copy(3 + 2 * level).start()

        s, w = T[:, 0:256], T[:, 256:512]
        cut_other = factor * dot3(p_oth[level], w)
        for k in range(3):
            passed(level, k).wait_recv()
        p = p_own[level]
        cut = dot3(p[:, 0:192], recv[level, 0:192, 256:512])
        direct(level, 3).wait_recv()
        for k in range(4):
            direct(level, k).wait_send()
            if k < 3:
                passed(level, k).wait_send()
        s = s - factor * (cut + dot3(p[:, 192:256], recv[level, 192:256, 256:512]))
        so = recv[level, :, 0:256] - cut_other
        M = jnp.concatenate([s, so], axis=0)
        mt = split(M.T)
        gram = dot3(mt, M)
        cross = dot3(mt, jnp.concatenate([w, recv[level, :, 256:512]], axis=0))
        trace = jnp.sum(jnp.where(eye, gram, 0.0))
        shift = 0.001 * (trace / 256.0 + 1e-6)
        T[:, 0:256] = gram + jnp.where(eye, shift, 0.0)
        T[:, 256:512] = cross
        T[:, 512:768] = jnp.where(eye, 1.0, 0.0)

        def after_block(k):
            @pl.when(level < 6)
            def _():
                direct(level + 1, k).start()
                if k >= 2:
                    direct(level + 1, k - 2).wait_recv()
                    passed(level + 1, k - 2).start()

            if k == 1:

                @pl.when(level < 2)
                def _():
                    p_step(3 + 2 * level)
                    p_copy(4 + 2 * level).start()

        eliminate(T, after_block)
        q = dot3(s, T[:, 512:768], NT)

        @pl.when(level == 0)
        def _():
            leaf_ref[...] = q

        @pl.when(level > 0)
        def _():
            upper_ref[level - 1] = q

        @pl.when(level < 6)
        def _():
            direct(level + 1, 2).wait_recv()
            passed(level + 1, 2).start()

        return carry

    lax.fori_loop(0, 7, level_body, 0)


def whole(front, keep, probes, coupling):
    vmem = pl.BlockSpec(memory_space=pltpu.VMEM)
    dma = pltpu.SemaphoreType.DMA
    return pl.pallas_call(
        whole_kernel,
        out_shape=[
            jax.ShapeDtypeStruct((256, 256), F32),
            jax.ShapeDtypeStruct((6, 256, 256), F32),
        ],
        in_specs=[pl.BlockSpec(memory_space=pl.ANY), vmem, vmem, vmem],
        out_specs=[vmem] * 2,
        scratch_shapes=[
            pltpu.VMEM((2048, 4096), BF),
            pltpu.VMEM((4096, 256), BF),
            pltpu.VMEM((2048, 256), F32),
            pltpu.VMEM((4, 256, 256), F32),
            pltpu.VMEM((3, 256, 256), F32),
            pltpu.VMEM((256, 256), BF),
            pltpu.VMEM((256, 768), F32),
            pltpu.VMEM((7, 256, 512), F32),
            pltpu.VMEM((7, 256, 256), F32),
            pltpu.VMEM((7, 256, 256), F32),
            dma((4,)), dma((2, 3)), dma((2, 3)), dma((2, 4, 3)), dma((2, 4, 3)),
            dma((4,)), dma((4,)), dma((3,)), dma((3,)), dma((4,)),
            dma((4,)), dma((7, 4)), dma((3,)), dma((7, 3)), dma((7,)), dma((7,)),
        ],
        compiler_params=pltpu.CompilerParams(
            collective_id=1, has_side_effects=True, vmem_limit_bytes=52 << 20
        ),
        cost_estimate=pl.CostEstimate(flops=1 << 32, bytes_accessed=1 << 24, transcendentals=0),
    )(front, keep, probes, coupling)


def shards(front, tile_mask, probes, coupling):
    row_index = lax.axis_index("row")
    col_index = lax.axis_index("col")
    tile_above = row_index * 8 + jnp.arange(8, dtype=jnp.int32)
    tile_across = col_index * 16 + jnp.arange(16, dtype=jnp.int32)
    keep = tile_mask * (tile_above[:, None] // 2 != tile_across[None, :] // 2).astype(jnp.int32)
    keep = jnp.repeat(keep.astype(F32), 256, axis=1)
    leaf, upper = whole(front, keep, probes, coupling)
    return leaf, upper


def solution(mesh):
    in_specs = (P("row", "col"), P("row", "col"), P(("col", "row"), None), P(("row", "col"), None))
    out_specs = (P(("row", "col"), None), P(None, ("row", "col"), None))
    return jax.shard_map(shards, mesh=mesh, in_specs=in_specs, out_specs=out_specs, check_vma=False)
```

time: 177 us -> 144 us (0.81)
  Pallas kernels: 172 us -> 137 us
  local copies, waits for them, and re-layouts: 2.9 us -> 5.44 us
    pallas_call x2 -> x1, Pallas kernels: 172 us -> 137 us  [whole(): pl.pallas_call(whole_kernel, out_shape=[jax.ShapeDtypeStruct((256, 256),...]
    unnamed x6, local copies, waits for them, and re-layouts: 2.75 us -> 5.29 us
where the time goes in v4:
time: 144 us
  Pallas kernels  137 us (95%)
  local copies, waits for them, and re-layouts  5.44 us (4%)
    pallas_call x1, Pallas kernels, whole(): pl.pallas_call(whole_kernel, out_shape=[jax.ShapeDtypeStruct((256, 256),...  137 us
    unnamed x6, local copies, waits for them, and re-layouts  5.29 us

profile of v4, /device:TPU:2, one launch (start us, length us, event | category | flops | bytes accessed | tf_op | source)
XLA Modules:
  0.0 143.8 jit_solution(13088890608658383104)
XLA Ops:
  0.7 0.8 select_convert_fusion
  1.4 0.1 copy.6
  1.5 0.1 broadcast_in_dim.2
  1.6 0.0 copy-start
  1.6 0.9 copy-done
  2.5 0.0 copy-start.1
  2.5 0.9 copy-done.1
  3.4 136.9 %shard_map.59 = (f32[256,256]{1,0:T(8,128)S(1)}, f32[6,256,256]{2,1,0:T(8,128)}) custom-call(bf16[2048,4096]{1,0:T(8,128)(2,1)} %front_ref.1, f32[8,4096]{1,0:T(8,128)S(1)} %bitcast.1, bf16[256,256]{1,0:T(8,128)(2,1)S(1)} %copy-done.1, f32[256,256]{1,0:T(8,128)S(1)} %copy-done), custom_call_target="tpu_custom_call" | custom-call | flops 4294967296 | bytes 16777216 | tf_op jit(solution)/shard_map/pallas_call | solution.py:388
  140.4 0.7 copy.9
  141.1 2.7 %copy.10 = f32[6,256,256]{2,1,0:T(8,128)} copy(f32[6,256,256]{2,1,0:T(8,128)} %get-tuple-element.5) | data formatting | bytes 3145728
  (2 shorter events, 0.0 us)
Async XLA Ops:
  1.6 1.0 copy-start
  2.5 0.9 copy-start.1

commit v5 on v4

--- a/solution.py
+++ b/solution.py
@@ -102,8 +102,8 @@
     return out
 
 
-def whole_kernel(front_ref, keep_ref, probes_ref, p_ref, leaf_ref, upper_ref,
-                 F, B, acc, from_core, from_x, leaf, T, recv, p_own, p_oth,
+def whole_kernel(front_ref, mask_ref, probes_ref, p_ref, leaf_ref, upper_ref,
+                 keep_ref, F, B, acc, from_core, from_x, leaf, T, recv, p_own, p_oth,
                  f_sem, near_send, near_recv, far_send, far_recv, c_send, c_recv, x_send, x_recv, l_sem,
                  d_send, d_recv, w_send, w_recv, p_send, p_recv):
     row, col = lax.axis_index("row"), lax.axis_index("col")
@@ -155,7 +155,7 @@
         return remote(acc.at[t], from_x.at[d - 1], x_send.at[d - 1], x_recv.at[d - 1], along_x(d, False))
 
     def to_leaf():
-        return remote(probes_ref, leaf, l_sem.at[0], l_sem.at[1], (target // 8, target % 8))
+        return remote(B.at[own], leaf, l_sem.at[0], l_sem.at[1], (target // 8, target % 8))
 
     def partner(level):
         h = 2**level if isinstance(level, int) else by_level(level, [1, 2, 4, 8, 16, 32, 64])
@@ -194,8 +194,18 @@
     pl.semaphore_signal(barrier, inc=1, device_id=source, device_id_type=MESH)
 
     own = pl.ds(pl.multiple_of(row * 256, 256), 256)
-    B[own, :] = probes_ref[...]
-    p_own[0] = p_ref[...]
+    fetch_probes = pltpu.make_async_copy(probes_ref, B.at[own], l_sem.at[4])
+    fetch_p = pltpu.make_async_copy(p_ref, p_own.at[0], l_sem.at[5])
+    fetch_probes.start()
+    fetch_p.start()
+    above = row * 8 + lax.broadcasted_iota(jnp.int32, (8, 16), 0)
+    across = col * 16 + lax.broadcasted_iota(jnp.int32, (8, 16), 1)
+    kept = jnp.where(above // 2 == across // 2, 0.0, mask_ref[...].astype(F32)).astype(BF)
+    spread = lax.broadcasted_iota(jnp.int32, (16, 4096), 1) // 256 == lax.broadcasted_iota(
+        jnp.int32, (16, 4096), 0
+    )
+    keep_ref[...] = jnp.dot(kept, spread.astype(BF), preferred_element_type=F32)
+    fetch_probes.wait()
     pl.semaphore_wait(barrier, 11)
 
     for d in (1, 3, 2):
@@ -204,6 +214,7 @@
     for d in (1, 3, 2):
         far(0, 0, d).start()
         far(1, 0, d).start()
+    fetch_p.wait()
     p_copy(0).start()
     for held in (1, 3, 2):
         near(0, held).wait_recv()
@@ -218,7 +229,7 @@
 
     @pl.when(jnp.logical_not(moved))
     def _():
-        leaf[...] = probes_ref[...]
+        leaf[...] = B[own, :]
 
     p_step(0)
     p_copy(1).start()
@@ -308,21 +319,8 @@
     columns = lax.broadcasted_iota(jnp.int32, (256, 256), 1)
     eye = rows == columns
 
-    def level_body(level, carry):
+    def level_body(level, early, last):
         factor = by_level(level, [0.0] + [2.0 ** (-l / 2.0) for l in range(1, 7)])
-
-        @pl.when(level == 1)
-        def _():
-            p_step(4)
-
-        @pl.when(level == 2)
-        def _():
-            p_copy(6).wait()
-
-        @pl.when(level < 2)
-        def _():
-            p_copy(3 + 2 * level).start()
-
         s, w = T[:, 0:256], T[:, 256:512]
         cut_other = factor * dot3(p_oth[level], w)
         for k in range(3):
@@ -347,43 +345,55 @@
         T[:, 512:768] = jnp.where(eye, 1.0, 0.0)
 
         def after_block(k):
-            @pl.when(level < 6)
-            def _():
+            if not last:
                 direct(level + 1, k).start()
                 if k >= 2:
                     direct(level + 1, k - 2).wait_recv()
                     passed(level + 1, k - 2).start()
-
-            if k == 1:
-
-                @pl.when(level < 2)
-                def _():
-                    p_step(3 + 2 * level)
-                    p_copy(4 + 2 * level).start()
+            if early and k == 1:
+                p_step(3 + 2 * level)
+                p_copy(4 + 2 * level).start()
 
         eliminate(T, after_block)
         q = dot3(s, T[:, 512:768], NT)
 
-        @pl.when(level == 0)
-        def _():
-            leaf_ref[...] = q
-
-        @pl.when(level > 0)
-        def _():
+        if early:
+
+            @pl.when(level == 0)
+            def _():
+                leaf_ref[...] = q
+
+            @pl.when(level > 0)
+            def _():
+                upper_ref[0] = q
+        else:
             upper_ref[level - 1] = q
-
-        @pl.when(level < 6)
-        def _():
+        if not last:
             direct(level + 1, 2).wait_recv()
             passed(level + 1, 2).start()
-
-        return carry
-
-    lax.fori_loop(0, 7, level_body, 0)
-
-
-def whole(front, keep, probes, coupling):
+        if early:
+            p_step(4 + 2 * level)
+
+            @pl.when(level == 0)
+            def _():
+                p_copy(5).start()
+
+    p_copy(3).start()
+
+    @pl.loop(0, 2)
+    def _(level):
+        level_body(level, True, False)
+
+    @pl.loop(2, 6)
+    def _(level):
+        level_body(level, False, False)
+
+    level_body(6, False, True)
+
+
+def whole(front, mask, probes, coupling):
     vmem = pl.BlockSpec(memory_space=pltpu.VMEM)
+    anywhere = pl.BlockSpec(memory_space=pltpu.HBM)
     dma = pltpu.SemaphoreType.DMA
     return pl.pallas_call(
         whole_kernel,
@@ -391,9 +401,10 @@
             jax.ShapeDtypeStruct((256, 256), F32),
             jax.ShapeDtypeStruct((6, 256, 256), F32),
         ],
-        in_specs=[pl.BlockSpec(memory_space=pl.ANY), vmem, vmem, vmem],
+        in_specs=[anywhere, vmem, anywhere, anywhere],
         out_specs=[vmem] * 2,
         scratch_shapes=[
+            pltpu.VMEM((8, 4096), F32),
             pltpu.VMEM((2048, 4096), BF),
             pltpu.VMEM((4096, 256), BF),
             pltpu.VMEM((2048, 256), F32),
@@ -402,27 +413,21 @@
             pltpu.VMEM((256, 256), BF),
             pltpu.VMEM((256, 768), F32),
             pltpu.VMEM((7, 256, 512), F32),
-            pltpu.VMEM((7, 256, 256), F32),
+            pltpu.VMEM((8, 256, 256), F32),
             pltpu.VMEM((7, 256, 256), F32),
             dma((4,)), dma((2, 3)), dma((2, 3)), dma((2, 4, 3)), dma((2, 4, 3)),
-            dma((4,)), dma((4,)), dma((3,)), dma((3,)), dma((4,)),
+            dma((4,)), dma((4,)), dma((3,)), dma((3,)), dma((6,)),
             dma((4,)), dma((7, 4)), dma((3,)), dma((7, 3)), dma((7,)), dma((7,)),
         ],
         compiler_params=pltpu.CompilerParams(
-            collective_id=1, has_side_effects=True, vmem_limit_bytes=52 << 20
+            collective_id=1, has_side_effects=True, vmem_limit_bytes=40 << 20
         ),
         cost_estimate=pl.CostEstimate(flops=1 << 32, bytes_accessed=1 << 24, transcendentals=0),
-    )(front, keep, probes, coupling)
+    )(front, mask, probes, coupling)
 
 
 def shards(front, tile_mask, probes, coupling):
-    row_index = lax.axis_index("row")
-    col_index = lax.axis_index("col")
-    tile_above = row_index * 8 + jnp.arange(8, dtype=jnp.int32)
-    tile_across = col_index * 16 + jnp.arange(16, dtype=jnp.int32)
-    keep = tile_mask * (tile_above[:, None] // 2 != tile_across[None, :] // 2).astype(jnp.int32)
-    keep = jnp.repeat(keep.astype(F32), 256, axis=1)
-    leaf, upper = whole(front, keep, probes, coupling)
+    leaf, upper = whole(front, tile_mask, probes, coupling)
     return leaf, upper
 
 

time: 144 us -> 142 us (0.986)
    unnamed x6 -> x8, local copies, waits for them, and re-layouts: 5.29 us -> 4.38 us
where the time goes in v5:
time: 142 us; the launch traced here: 141 us
  Pallas kernels  136 us (96%)
  local copies, waits for them, and re-layouts  4.38 us (3%)
    pallas_call x1, Pallas kernels, whole(): pl.pallas_call(whole_kernel, out_shape=[jax.ShapeDtypeStruct((256, 256),...  136 us
    unnamed x8, local copies, waits for them, and re-layouts  4.38 us

profile of v5, /device:TPU:2, one launch (start us, length us, event | category | flops | bytes accessed | tf_op | source)
XLA Modules:
  0.0 141.0 jit_solution(4550372342090759323)
XLA Ops:
  0.6 0.0 copy-start
  0.6 0.9 copy-done
  1.6 0.0 copy-start.1
  1.6 0.9 copy-done.1
  2.5 0.0 copy-start.2
  2.5 0.7 copy-done.2
  3.2 135.9 %shard_map.59 = (f32[256,256]{1,0:T(8,128)S(1)}, f32[6,256,256]{2,1,0:T(8,128)S(1)}) custom-call(bf16[2048,4096]{1,0:T(8,128)(2,1)} %front_ref.1, s32[8,16]{1,0:T(8,128)S(1)} %copy-done.2, bf16[256,256]{1,0:T(8,128)(2,1)S(1)} %copy-done.1, f32[256,256]{1,0:T(8,128)S(1)} %copy-done), custom_call_target="tpu_custom_call" | custom-call | flops 4294967296 | bytes 16777216 | tf_op jit(solution)/shard_map/pallas_call | solution.py:398
  139.1 0.7 copy.8
  139.8 1.1 copy.9
Async XLA Ops:
  0.6 1.0 copy-start
  1.6 0.9 copy-start.1
  2.5 0.7 copy-start.2

commit v6 on v5

--- a/solution.py
+++ b/solution.py
@@ -103,8 +103,8 @@
 
 
 def whole_kernel(front_ref, mask_ref, probes_ref, p_ref, leaf_ref, upper_ref,
-                 keep_ref, F, B, acc, from_core, from_x, leaf, T, recv, p_own, p_oth,
-                 f_sem, near_send, near_recv, far_send, far_recv, c_send, c_recv, x_send, x_recv, l_sem,
+                 keep_ref, F, B, acc, from_core, from_x, relayed, leaf, T, recv, p_own, p_oth,
+                 f_sem, near_send, near_recv, far_send, far_recv, c_send, c_recv, x_send, x_recv, r_send, r_recv, l_sem,
                  d_send, d_recv, w_send, w_recv, p_send, p_recv):
     row, col = lax.axis_index("row"), lax.axis_index("col")
     z, y = row // 4, row % 4
@@ -150,9 +150,17 @@
         t = pl.ds(pl.multiple_of(((x + d) % 4 * 2 + 1 - c) * 256, 256), 256)
         return remote(acc.at[t], from_core.at[d], c_send.at[d], c_recv.at[d], along_x(0, True))
 
-    def to_x(d):
-        t = pl.ds(pl.multiple_of(((x + d) % 4 * 2 + c) * 256, 256), 256)
-        return remote(acc.at[t], from_x.at[d - 1], x_send.at[d - 1], x_recv.at[d - 1], along_x(d, False))
+    def tile_rows(d, h):
+        return pl.ds(pl.multiple_of(((x + d) % 4 * 2 + c) * 256 + h * 128, 128), 128)
+
+    def relay(d):
+        i = 0 if d == 1 else 1
+        return remote(acc.at[tile_rows(2, 1 - i)], relayed.at[i], r_send.at[i], r_recv.at[i], along_x(d, False))
+
+    def to_x(d, h):
+        i = 0 if d == 1 else 1
+        return remote(acc.at[tile_rows(d, h)], from_x.at[i, pl.ds(h * 128, 128)],
+                      x_send.at[i, h], x_recv.at[i, h], along_x(d, False))
 
     def to_leaf():
         return remote(B.at[own], leaf, l_sem.at[0], l_sem.at[1], (target // 8, target % 8))
@@ -266,8 +274,11 @@
         to_core(e).wait_recv()
         r = pl.ds(pl.multiple_of(((x + e) % 4 * 2 + c) * 256, 256), 256)
         acc[r, :] = acc[r, :] + from_core[e]
-        if e:
-            to_x(e).start()
+        if e == 2:
+            relay(1).start()
+            relay(3).start()
+        elif e:
+            to_x(e, 0 if e == 1 else 1).start()
 
     ahead = None
     for e in (2, 1, 3, 0):
@@ -281,10 +292,14 @@
             finish(ahead)
         ahead = e
     finish(0)
-    total = acc[pl.ds(pl.multiple_of(col * 256, 256), 256), :]
-    for d in (1, 3, 2):
-        to_x(d).wait_recv()
-        total = total + from_x[d - 1]
+    for d, h, i in ((1, 1, 0), (3, 0, 1)):
+        relay(d).wait_recv()
+        r = tile_rows(d, h)
+        acc[r, :] = acc[r, :] + relayed[i]
+        to_x(d, h).start()
+    for d, h in ((1, 0), (3, 1), (1, 1), (3, 0)):
+        to_x(d, h).wait_recv()
+    total = acc[pl.ds(pl.multiple_of(col * 256, 256), 256), :] + (from_x[0] + from_x[1])
     p_step(2)
     T[:, 0:256] = total
 
@@ -309,8 +324,10 @@
                 far(h, held, d).wait_send()
     for d in range(4):
         to_core(d).wait_send()
-    for d in (1, 2, 3):
-        to_x(d).wait_send()
+    for d in (1, 3):
+        relay(d).wait_send()
+        to_x(d, 0).wait_send()
+        to_x(d, 1).wait_send()
     corner.wait()
     for k in range(3):
         direct(0, k).wait_recv()
@@ -409,14 +426,15 @@
             pltpu.VMEM((4096, 256), BF),
             pltpu.VMEM((2048, 256), F32),
             pltpu.VMEM((4, 256, 256), F32),
-            pltpu.VMEM((3, 256, 256), F32),
+            pltpu.VMEM((2, 256, 256), F32),
+            pltpu.VMEM((2, 128, 256), F32),
             pltpu.VMEM((256, 256), BF),
             pltpu.VMEM((256, 768), F32),
             pltpu.VMEM((7, 256, 512), F32),
             pltpu.VMEM((8, 256, 256), F32),
             pltpu.VMEM((7, 256, 256), F32),
             dma((4,)), dma((2, 3)), dma((2, 3)), dma((2, 4, 3)), dma((2, 4, 3)),
-            dma((4,)), dma((4,)), dma((3,)), dma((3,)), dma((6,)),
+            dma((4,)), dma((4,)), dma((2, 2)), dma((2, 2)), dma((2,)), dma((2,)), dma((6,)),
             dma((4,)), dma((7, 4)), dma((3,)), dma((7, 3)), dma((7,)), dma((7,)),
         ],
         compiler_params=pltpu.CompilerParams(

time: 142 us -> 139 us (0.979)
  Pallas kernels: 136 us -> 134 us
    pallas_call x1, Pallas kernels: 136 us -> 134 us  [whole(): pl.pallas_call(whole_kernel, out_shape=[jax.ShapeDtypeStruct((256, 256),...]
where the time goes in v6:
time: 139 us
  Pallas kernels  134 us (96%)
  local copies, waits for them, and re-layouts  4.38 us (3%)
    pallas_call x1, Pallas kernels, whole(): pl.pallas_call(whole_kernel, out_shape=[jax.ShapeDtypeStruct((256, 256),...  134 us
    unnamed x8, local copies, waits for them, and re-layouts  4.38 us

profile of v6, /device:TPU:2, one launch (start us, length us, event | category | flops | bytes accessed | tf_op | source)
XLA Modules:
  0.0 139.0 jit_solution(2099725278922608041)
XLA Ops:
  0.6 0.0 copy-start
  0.6 0.9 copy-done
  1.6 0.0 copy-start.1
  1.6 0.9 copy-done.1
  2.5 0.0 copy-start.2
  2.5 0.7 copy-done.2
  3.2 134.0 %shard_map.59 = (f32[256,256]{1,0:T(8,128)S(1)}, f32[6,256,256]{2,1,0:T(8,128)S(1)}) custom-call(bf16[2048,4096]{1,0:T(8,128)(2,1)} %front_ref.1, s32[8,16]{1,0:T(8,128)S(1)} %copy-done.2, bf16[256,256]{1,0:T(8,128)(2,1)S(1)} %copy-done.1, f32[256,256]{1,0:T(8,128)S(1)} %copy-done), custom_call_target="tpu_custom_call" | custom-call | flops 4294967296 | bytes 16777216 | tf_op jit(solution)/shard_map/pallas_call | solution.py:415
  137.1 0.7 copy.8
  137.9 1.1 copy.9
Async XLA Ops:
  0.6 1.0 copy-start
  1.6 0.9 copy-start.1
  2.5 0.7 copy-start.2

commit v7 on v6

--- a/solution.py
+++ b/solution.py
@@ -344,11 +344,11 @@
             passed(level, k).wait_recv()
         p = p_own[level]
         cut = dot3(p[:, 0:192], recv[level, 0:192, 256:512])
+        for k in range(3):
+            direct(level, k).wait_send()
+            passed(level, k).wait_send()
         direct(level, 3).wait_recv()
-        for k in range(4):
-            direct(level, k).wait_send()
-            if k < 3:
-                passed(level, k).wait_send()
+        direct(level, 3).wait_send()
         s = s - factor * (cut + dot3(p[:, 192:256], recv[level, 192:256, 256:512]))
         so = recv[level, :, 0:256] - cut_other
         M = jnp.concatenate([s, so], axis=0)
@@ -364,9 +364,10 @@
         def after_block(k):
             if not last:
                 direct(level + 1, k).start()
-                if k >= 2:
-                    direct(level + 1, k - 2).wait_recv()
-                    passed(level + 1, k - 2).start()
+                if k == 3:
+                    for early_k in range(2):
+                        direct(level + 1, early_k).wait_recv()
+                        passed(level + 1, early_k).start()
             if early and k == 1:
                 p_step(3 + 2 * level)
                 p_copy(4 + 2 * level).start()

time: 139 us -> 137 us (0.986); the launches traced: 139 us -> 135 us
  Pallas kernels: 134 us -> 130 us
    pallas_call x1, Pallas kernels: 134 us -> 130 us  [whole(): pl.pallas_call(whole_kernel, out_shape=[jax.ShapeDtypeStruct((256, 256),...]
where the time goes in v7:
time: 137 us; the launch traced here: 135 us
  Pallas kernels  130 us (95%)
  local copies, waits for them, and re-layouts  4.38 us (3%)
    pallas_call x1, Pallas kernels, whole(): pl.pallas_call(whole_kernel, out_shape=[jax.ShapeDtypeStruct((256, 256),...  130 us
    unnamed x8, local copies, waits for them, and re-layouts  4.38 us

profile of v7, /device:TPU:2, one launch (start us, length us, event | category | flops | bytes accessed | tf_op | source)
XLA Modules:
  0.0 134.7 jit_solution(12334275992129329859)
XLA Ops:
  0.6 0.0 copy-start
  0.6 0.9 copy-done
  1.6 0.0 copy-start.1
  1.6 0.9 copy-done.1
  2.5 0.0 copy-start.2
  2.5 0.7 copy-done.2
  3.2 129.7 %shard_map.59 = (f32[256,256]{1,0:T(8,128)S(1)}, f32[6,256,256]{2,1,0:T(8,128)S(1)}) custom-call(bf16[2048,4096]{1,0:T(8,128)(2,1)} %front_ref.1, s32[8,16]{1,0:T(8,128)S(1)} %copy-done.2, bf16[256,256]{1,0:T(8,128)(2,1)S(1)} %copy-done.1, f32[256,256]{1,0:T(8,128)S(1)} %copy-done), custom_call_target="tpu_custom_call" | custom-call | flops 4294967296 | bytes 16777216 | tf_op jit(solution)/shard_map/pallas_call | solution.py:416
  132.8 0.7 copy.8
  133.5 1.1 copy.9
Async XLA Ops:
  0.6 1.0 copy-start
  1.6 0.9 copy-start.1
  2.5 0.7 copy-start.2
